TPU v7x, 256 devices: a whole 4x4x8 slice. The times are simulated.
256 devices in a mesh: ctx: 128 (over z, y, x), head: 2 (over core).
Axes of the slice: x: 4, y: 4, z: 8, core: 2. Of those that a mesh axis runs over, the one named last changes fastest.
Arguments:
- queries: bfloat16 [32768, 3072], P(('ctx', 'head')), may hold values from -30 to 30
- keys: bfloat16 [32768, 3072], P(('ctx', 'head')), may hold values from -30 to 30
- values: bfloat16 [32768, 3072], P(('ctx', 'head')), may hold values from -6 to 6
- clip_ids: int32 [32768], P('ctx'), may hold values from 0 to 63, never falling along the last dimension, each value on 1 to 1024 neighbouring positions
- group_ids: int32 [32768], P('ctx'), may hold values from 0 to 511, never falling along the last dimension, each value on 1 to 128 neighbouring positions
- pair_kinds: int32 [128, 4], P('ctx'), may hold values from 0 to 2, as said below
Outputs:
- attended: bfloat16 [32768, 3072], P(('ctx', 'head'))
Inputs may be any that keep to these rules, and one draw needn't show every extreme that they name: `pair_kinds`: entries are 0 (block not read), 1 (same clip, earlier or equal group) or 2 (every key of the block).
All inputs are finite; a program needn't handle non-finite values.
Results may differ from a plain program's by a relative error of at most 0.009.
Values may be sent and summed in bfloat16 or wider, within the bound.
A program may use at most 64 MiB of HBM per device.

v0:
```python
import jax
import jax.numpy as jnp
from jax import lax
from jax.sharding import PartitionSpec as P

HD = 128
WIN = 4


def passed_along(value, axis, steps):
    count = lax.axis_size(axis)
    initial, last = (max(0, -steps), min(count, count - steps))
    return lax.ppermute(value, axis, [(source, source + steps) for source in range(initial, last)])


def attend_block(state, query_rows, key_rows, value_rows, allowed):
    highest, row_total, output = state
    scores = jnp.einsum(
        "qhd,khd->hqk", query_rows, key_rows, preferred_element_type=jnp.float32
    ) * HD ** (-0.5)
    scores = jnp.where(allowed[None], scores, -1e30)
    fresh = jnp.maximum(highest, jnp.max(scores, axis=-1))
    weights = jnp.where(allowed[None], jnp.exp(scores - fresh[:, :, None]), 0.0)
    shrink = jnp.exp(highest - fresh)
    row_total = row_total * shrink + jnp.sum(weights, axis=-1)
    output = output * jnp.transpose(shrink)[:, :, None] + jnp.einsum(
        "hqk,khd->qhd", weights.astype(jnp.bfloat16), value_rows, preferred_element_type=jnp.float32
    )
    return (fresh, row_total, output)


def shards(queries, keys, values, clip_ids, group_ids, pair_kinds):
    local_rows = queries.shape[0]
    head_count = queries.shape[1] // HD
    query_in = queries.reshape(local_rows, head_count, HD)
    key_in = keys.reshape(local_rows, head_count, HD)
    value_in = values.reshape(local_rows, head_count, HD)
    query_rows, key_rows, value_rows = (
        lax.all_to_all(query_in, "head", split_axis=1, concat_axis=0, tiled=True),
        lax.all_to_all(key_in, "head", split_axis=1, concat_axis=0, tiled=True),
        lax.all_to_all(value_in, "head", split_axis=1, concat_axis=0, tiled=True),
    )
    rows_now = query_rows.shape[0]
    local_heads = query_rows.shape[1]

    def allowed_for(key_clip, key_group):
        return (clip_ids[:, None] == key_clip[None, :]) & (key_group[None, :] <= group_ids[:, None])

    state = (
        jnp.full((local_heads, rows_now), -1e30, jnp.float32),
        jnp.zeros((local_heads, rows_now), jnp.float32),
        jnp.zeros((rows_now, local_heads, HD), jnp.float32),
    )
    state = attend_block(state, query_rows, key_rows, value_rows, allowed_for(clip_ids, group_ids))
    position = lax.axis_index("ctx")
    kind_codes = pair_kinds[0]
    carried = (key_rows, value_rows, clip_ids, group_ids)
    for offset in range(1, WIN + 1):
        carried = passed_along((carried[0], carried[1], carried[2], carried[3]), "ctx", 1)
        arrived = carried
        kind_code = kind_codes[offset - 1]
        live = (kind_code > 0) & (position - offset >= 0)
        allowed = jnp.logical_or(kind_code == 2, allowed_for(arrived[2], arrived[3]))
        state = lax.cond(
            live,
            lambda current: attend_block(current, query_rows, arrived[0], arrived[1], allowed),
            lambda current: current,
            state,
        )
    highest, row_total, output = state
    result = (output / jnp.transpose(row_total)[:, :, None]).astype(jnp.bfloat16)
    returned = lax.all_to_all(result, "head", split_axis=0, concat_axis=1, tiled=True)
    return returned.reshape(local_rows, head_count * HD)


def solution(mesh):
    in_specs = (
        P(("ctx", "head"), None),
        P(("ctx", "head"), None),
        P(("ctx", "head"), None),
        P("ctx"),
        P("ctx"),
        P("ctx", None),
    )
    out_specs = P(("ctx", "head"), None)
    return jax.shard_map(shards, mesh=mesh, in_specs=in_specs, out_specs=out_specs, check_vma=False)
```

profile of v0, /device:TPU:121, one launch (start us, length us, event | category | flops | bytes accessed | tf_op | source)
XLA Modules:
  0.0 206.7 jit_solution(9885593922442822416)
XLA Ops:
  0.0 2.4 %copy.45 = bf16[128,3072]{0,1:T(8,128)(2,1)} copy(bf16[128,3072]{1,0:T(8,128)(2,1)} %param.15) | data formatting | bytes 1572864 | tf_op args[1]
  2.4 4.2 %all-to-all-start.1 = ((bf16[128,24,128]{0,2,1:T(8,128)(2,1)}), bf16[128,24,128]{0,2,1:T(8,128)(2,1)S(1)}, u32[]{:S(2)}, u32[]{:S(2)}) async-start(bf16[128,24,128]{0,2,1:T(8,128)(2,1)} %bitcast.17), calls=%async_computation.1 | async-start | bytes 1572864 | tf_op jit(solution)/shard_map/all_to_all | solution.py:40
  6.6 1.2 copy.48
  8.1 3.9 %all-to-all-start.2 = ((bf16[128,24,128]{0,2,1:T(8,128)(2,1)}), bf16[128,24,128]{0,2,1:T(8,128)(2,1)S(1)}, u32[]{:S(2)}, u32[]{:S(2)}) async-start(bf16[128,24,128]{0,2,1:T(8,128)(2,1)} %bitcast.23), calls=%async_computation.2 | async-start | bytes 1572864 | tf_op jit(solution)/shard_map/all_to_all | solution.py:41
  12.4 3.1 %collective-permute-start.2 = (bf16[256,12,128]{2,0,1:T(8,128)(2,1)S(1)}, bf16[256,12,128]{2,0,1:T(8,128)(2,1)}, u32[]{:S(2)}, u32[]{:S(2)}) collective-permute-start(bf16[256,12,128]{2,0,1:T(8,128)(2,1)S(1)} %bitcast.67), channel_id=1, source_target_pairs={{0,2},{2,4},{4,6},{6,8},{8,10},{10,12},{12,14},{14,16},{16,18},{18... | collective-permute-start | bytes 2359304 | tf_op jit(solution)/shard_map/ppermute | solution.py:13
  15.9 3.1 %collective-permute-start.3 = (bf16[256,12,128]{2,0,1:T(8,128)(2,1)S(1)}, bf16[256,12,128]{2,0,1:T(8,128)(2,1)}, u32[]{:S(2)}, u32[]{:S(2)}) collective-permute-start(bf16[256,12,128]{2,0,1:T(8,128)(2,1)S(1)} %bitcast.73), channel_id=1, source_target_pairs={{0,2},{2,4},{4,6},{6,8},{8,10},{10,12},{12,14},{14,16},{16,18},{18... | collective-permute-start | bytes 2359304 | tf_op jit(solution)/shard_map/ppermute | solution.py:13
  19.1 16.6 %collective-permute-done.2 = bf16[256,12,128]{2,0,1:T(8,128)(2,1)} collective-permute-done((bf16[256,12,128]{2,0,1:T(8,128)(2,1)S(1)}, bf16[256,12,128]{2,0,1:T(8,128)(2,1)}, u32[]{:S(2)}, u32[]{:S(2)}) %collective-permute-start.2) | collective-permute-done | bytes 786464 | tf_op jit(solution)/shard_map/ppermute | solution.py:13
  35.7 1.9 collective-permute-start.6
  37.6 14.9 %collective-permute-done.3 = bf16[256,12,128]{2,0,1:T(8,128)(2,1)} collective-permute-done((bf16[256,12,128]{2,0,1:T(8,128)(2,1)S(1)}, bf16[256,12,128]{2,0,1:T(8,128)(2,1)}, u32[]{:S(2)}, u32[]{:S(2)}) %collective-permute-start.3) | collective-permute-done | bytes 786464 | tf_op jit(solution)/shard_map/ppermute | solution.py:13
  52.5 1.9 collective-permute-start.7
  54.4 2.2 %collective-permute-start.1 = (s32[256]{0:T(256)S(1)}, s32[256]{0:T(256)S(1)}, u32[]{:S(2)}, u32[]{:S(2)}) collective-permute-start(s32[256]{0:T(256)S(1)} %copy-done.5), channel_id=1, source_target_pairs={{0,2},{2,4},{4,6},{6,8},{8,10},{10,12},{12,14},{14,16},{16,18},{18... | collective-permute-start | bytes 3080 | tf_op jit(solution)/shard_map/ppermute | solution.py:13
  56.7 2.9 %collective-permute-start = (s32[256]{0:T(256)S(1)}, s32[256]{0:T(256)S(1)}, u32[]{:S(2)}, u32[]{:S(2)}) collective-permute-start(s32[256]{0:T(256)S(1)} %copy-done.4), channel_id=1, source_target_pairs={{0,2},{2,4},{4,6},{6,8},{8,10},{10,12},{12,14},{14,16},{16,18},{18... | collective-permute-start | bytes 3080 | tf_op jit(solution)/shard_map/ppermute | solution.py:13
  59.6 2.3 %copy.42 = bf16[128,3072]{0,1:T(8,128)(2,1)} copy(bf16[128,3072]{1,0:T(8,128)(2,1)} %param.14) | data formatting | bytes 1572864 | tf_op args[0]
  61.9 5.6 %all-to-all-start = ((bf16[128,24,128]{0,2,1:T(8,128)(2,1)}), bf16[128,24,128]{0,2,1:T(8,128)(2,1)S(1)}, u32[]{:S(2)}, u32[]{:S(2)}) async-start(bf16[128,24,128]{0,2,1:T(8,128)(2,1)} %bitcast.12), calls=%async_computation | async-start | bytes 1572864 | tf_op jit(solution)/shard_map/all_to_all | solution.py:39
  72.1 14.1 %collective-permute-done.1 = s32[256]{0:T(256)S(1)} collective-permute-done((s32[256]{0:T(256)S(1)}, s32[256]{0:T(256)S(1)}, u32[]{:S(2)}, u32[]{:S(2)}) %collective-permute-start.1) | collective-permute-done | bytes 1056 | tf_op jit(solution)/shard_map/ppermute | solution.py:13
  86.2 1.9 collective-permute-start.5
  88.2 2.2 %collective-permute-start.4 = (s32[256]{0:T(256)S(1)}, s32[256]{0:T(256)S(1)}, u32[]{:S(2)}, u32[]{:S(2)}) collective-permute-start(s32[256]{0:T(256)S(1)} %collective-permute-done), channel_id=1, source_target_pairs={{0,2},{2,4},{4,6},{6,8},{8,10},{10,12},{12,14},{14,16},{16,18},{18... | collective-permute-start | bytes 3080 | tf_op jit(solution)/shard_map/ppermute | solution.py:13
  90.8 3.0 %collective-permute-start.10 = (bf16[256,12,128]{2,0,1:T(8,128)(2,1)S(1)}, bf16[256,12,128]{2,0,1:T(8,128)(2,1)}, u32[]{:S(2)}, u32[]{:S(2)}) collective-permute-start(bf16[256,12,128]{2,0,1:T(8,128)(2,1)S(1)} %collective-permute-done.6), channel_id=1, source_target_pairs={{0,2},{2,4},{4,6},{6,8},{8,10},{10,12},{12,14},{14,16},{16,18},{18... | collective-permute-start | bytes 2359304 | tf_op jit(solution)/shard_map/ppermute | solution.py:13
  93.8 9.6 %collective-permute-start.11 = (bf16[256,12,128]{2,0,1:T(8,128)(2,1)}, bf16[256,12,128]{2,0,1:T(8,128)(2,1)}, u32[]{:S(2)}, u32[]{:S(2)}) collective-permute-start(bf16[256,12,128]{2,0,1:T(8,128)(2,1)} %collective-permute-done.7), channel_id=1, source_target_pairs={{0,2},{2,4},{4,6},{6,8},{8,10},{10,12},{12,14},{14,16},{16,18},{18... | collective-permute-start | bytes 2359304 | tf_op jit(solution)/shard_map/ppermute | solution.py:13
  104.4 8.2 %collective-permute-done.10 = bf16[256,12,128]{2,0,1:T(8,128)(2,1)} collective-permute-done((bf16[256,12,128]{2,0,1:T(8,128)(2,1)S(1)}, bf16[256,12,128]{2,0,1:T(8,128)(2,1)}, u32[]{:S(2)}, u32[]{:S(2)}) %collective-permute-start.10) | collective-permute-done | bytes 786464 | tf_op jit(solution)/shard_map/ppermute | solution.py:13
  112.6 6.3 %collective-permute-start.14 = (bf16[256,12,128]{2,0,1:T(8,128)(2,1)}, bf16[256,12,128]{2,0,1:T(8,128)(2,1)}, u32[]{:S(2)}, u32[]{:S(2)}) collective-permute-start(bf16[256,12,128]{2,0,1:T(8,128)(2,1)} %collective-permute-done.10), channel_id=1, source_target_pairs={{0,2},{2,4},{4,6},{6,8},{8,10},{10,12},{12,14},{14,16},{16,18},{18... | collective-permute-start | bytes 2359304 | tf_op jit(solution)/shard_map/ppermute | solution.py:13
  118.8 10.6 %collective-permute-done.11 = bf16[256,12,128]{2,0,1:T(8,128)(2,1)} collective-permute-done((bf16[256,12,128]{2,0,1:T(8,128)(2,1)}, bf16[256,12,128]{2,0,1:T(8,128)(2,1)}, u32[]{:S(2)}, u32[]{:S(2)}) %collective-permute-start.11) | collective-permute-done | bytes 786464 | tf_op jit(solution)/shard_map/ppermute | solution.py:13
  129.4 6.4 %collective-permute-start.15 = (bf16[256,12,128]{2,0,1:T(8,128)(2,1)}, bf16[256,12,128]{2,0,1:T(8,128)(2,1)}, u32[]{:S(2)}, u32[]{:S(2)}) collective-permute-start(bf16[256,12,128]{2,0,1:T(8,128)(2,1)} %collective-permute-done.11), channel_id=1, source_target_pairs={{0,2},{2,4},{4,6},{6,8},{8,10},{10,12},{12,14},{14,16},{16,18},{18... | collective-permute-start | bytes 2359304 | tf_op jit(solution)/shard_map/ppermute | solution.py:13
  135.8 0.8 fusion.66
  136.6 4.1 %collective-permute-start.8 = (s32[256]{0:T(256)S(1)}, s32[256]{0:T(256)}, u32[]{:S(2)}, u32[]{:S(2)}) collective-permute-start(s32[256]{0:T(256)S(1)} %collective-permute-done.4), channel_id=1, source_target_pairs={{0,2},{2,4},{4,6},{6,8},{8,10},{10,12},{12,14},{14,16},{16,18},{18... | collective-permute-start | bytes 3080 | tf_op jit(solution)/shard_map/ppermute | solution.py:13
  140.7 2.2 %collective-permute-start.9 = (s32[256]{0:T(256)S(1)}, s32[256]{0:T(256)}, u32[]{:S(2)}, u32[]{:S(2)}) collective-permute-start(s32[256]{0:T(256)S(1)} %collective-permute-done.5), channel_id=1, source_target_pairs={{0,2},{2,4},{4,6},{6,8},{8,10},{10,12},{12,14},{14,16},{16,18},{18... | collective-permute-start | bytes 3080 | tf_op jit(solution)/shard_map/ppermute | solution.py:13
  142.9 1.3 bitcast_add_fusion.4
  144.3 18.9 %collective-permute-done.8 = s32[256]{0:T(256)} collective-permute-done((s32[256]{0:T(256)S(1)}, s32[256]{0:T(256)}, u32[]{:S(2)}, u32[]{:S(2)}) %collective-permute-start.8) | collective-permute-done | bytes 1056 | tf_op jit(solution)/shard_map/ppermute | solution.py:13
  163.1 6.3 %collective-permute-start.12 = (s32[256]{0:T(256)}, s32[256]{0:T(256)S(1)}, u32[]{:S(2)}, u32[]{:S(2)}) collective-permute-start(s32[256]{0:T(256)} %collective-permute-done.8), channel_id=1, source_target_pairs={{0,2},{2,4},{4,6},{6,8},{8,10},{10,12},{12,14},{14,16},{16,18},{18... | collective-permute-start | bytes 3080 | tf_op jit(solution)/shard_map/ppermute | solution.py:13
  169.5 4.1 %collective-permute-start.13 = (s32[256]{0:T(256)}, s32[256]{0:T(256)S(1)}, u32[]{:S(2)}, u32[]{:S(2)}) collective-permute-start(s32[256]{0:T(256)} %collective-permute-done.9), channel_id=1, source_target_pairs={{0,2},{2,4},{4,6},{6,8},{8,10},{10,12},{12,14},{14,16},{16,18},{18... | collective-permute-start | bytes 3080 | tf_op jit(solution)/shard_map/ppermute | solution.py:13
  173.6 5.2 %conditional.4 = ((f32[12,256]{1,0:T(8,128)S(1)}, f32[12,256]{1,0:T(8,128)S(1)}, f32[256,12,128]{2,0,1:T(8,128)S(1)})) conditional(s32[]{:T(128)} %convert_element_type.33, (f32[12,256]{1,0:T(8,128)S(1)}, f32[12,256]{1,0:T(8,128)S(1)}, f32[256,12,128]{2,0,1:T(8,128)S(1)}) %tuple.31, (pred[256,256]{0,1:T(8,128)(4,1)S(1)}, ...), branch_computations={%region_2.3_spmd, %region_3.6_spmd} | conditional | flops 413672448 | bytes 15335456 | solution.py:64
  173.6 1.7 fusion
  175.4 0.8 fusion.2
  176.2 2.6 %bitcast_add_fusion = f32[256,12,128]{2,0,1:T(8,128)S(1)} fusion(f32[256,12,128]{2,0,1:T(8,128)S(1)} %get-tuple-element.122, bf16[256,12,128]{2,0,1:T(8,128)(2,1)} %get-tuple-element.123, f32[12,256,256]{1,2,0:T(8,128)S(1)} %get-tuple-element.187, f32[12,256]{1,0:T(8,128)S(1)} %get-tuple-element.208, pred[256,256]{0,1:T(8,128)(4,1)S(1)} %get-tuple-element.118, ...), kind=kOutput, calls=%fused_computation.6 | convolution fusion | flops 206045184 | bytes 7168000 | tf_op jit(solution)/shard_map/cond/branch_1_fun/hqk,khd->qhd/dot_general | solution.py:26
  178.8 4.0 %conditional.5 = ((f32[12,256]{1,0:T(8,128)S(1)}, f32[12,256]{1,0:T(8,128)S(1)}, f32[256,12,128]{2,0,1:T(8,128)S(1)})) conditional(s32[]{:T(128)} %convert_element_type.32, (f32[12,256]{1,0:T(8,128)S(1)}, f32[12,256]{1,0:T(8,128)S(1)}, f32[256,12,128]{2,0,1:T(8,128)S(1)}) %get-tuple-element.227, (pred[256,256]{0,1:T(8,128)(4,1)S(1)}, ...), branch_computations={%region_6.7_spmd, %region_7.10_spmd} | conditional | flops 413672448 | bytes 15335456 | solution.py:64
  179.5 0.8 fusion.18
  180.3 2.6 %bitcast_add_fusion.1 = f32[256,12,128]{2,0,1:T(8,128)S(1)} fusion(f32[256,12,128]{2,0,1:T(8,128)S(1)} %get-tuple-element.129, bf16[256,12,128]{2,0,1:T(8,128)(2,1)} %get-tuple-element.130, f32[12,256,256]{1,2,0:T(8,128)S(1)} %get-tuple-element.189, f32[12,256]{1,0:T(8,128)S(1)} %get-tuple-element.214, pred[256,256]{0,1:T(8,128)(4,1)S(1)} %get-tuple-element.125, ...), kind=kOutput, calls=%fused_computation.24 | convolution fusion | flops 206045184 | bytes 7168000 | tf_op jit(solution)/shard_map/cond/branch_1_fun/hqk,khd->qhd/dot_general | solution.py:26
  182.9 6.8 %conditional.6 = ((f32[12,256]{1,0:T(8,128)S(1)}, f32[12,256]{1,0:T(8,128)S(1)}, f32[256,12,128]{2,0,1:T(8,128)S(1)})) conditional(s32[]{:T(128)} %convert_element_type.31, (f32[12,256]{1,0:T(8,128)S(1)}, f32[12,256]{1,0:T(8,128)S(1)}, f32[256,12,128]{2,0,1:T(8,128)S(1)}) %get-tuple-element.228, (s32[]{:T(128)}, s32[256]{0:T(256)}, ...), branch_computations={%region_10.11_spmd, %region_11.14_spmd} | conditional | flops 413934592 | bytes 15927338 | solution.py:64
  183.7 0.8 and_or_fusion
  184.6 1.8 fusion.32
  187.1 2.6 %bitcast_add_fusion.2 = f32[256,12,128]{2,0,1:T(8,128)S(1)} fusion(f32[256,12,128]{2,0,1:T(8,128)S(1)} %get-tuple-element.140, bf16[256,12,128]{2,0,1:T(8,128)(2,1)} %get-tuple-element.141, f32[12,256,256]{1,2,0:T(8,128)S(1)} %get-tuple-element.191, f32[12,256]{1,0:T(8,128)S(1)} %get-tuple-element.220, pred[256,256]{0,1:T(8,128)(4,1)S(1)} %and_or_fusion, ...), kind=kOutput, calls=%fused_computation.42 | convolution fusion | flops 206045184 | bytes 7168000 | tf_op jit(solution)/shard_map/cond/branch_1_fun/hqk,khd->qhd/dot_general | solution.py:26
  189.8 7.0 %conditional.7 = (f32[12,256]{1,0:T(8,128)S(1)}, f32[256,12,128]{2,1,0:T(8,128)S(1)}) conditional(s32[]{:T(128)} %convert_element_type.30, (f32[12,256]{1,0:T(8,128)S(1)}, f32[256,12,128]{2,0,1:T(8,128)S(1)}) %tuple.35, (s32[]{:T(128)}, s32[256]{0:T(256)S(1)}, s32[256,256]{0,1:T(8,128)S(1)}, s32[256]{0:T(256)S(1)}, s32[256,256]{0,1:T(8,128)S(1)}, ...), branch_computations={%region_14.15_spmd, %region_15.18_spmd} | conditional | flops 413934592 | bytes 19048474 | solution.py:64
  190.6 1.8 fusion.48
  193.2 2.6 %bitcast_add_fusion.3 = f32[256,12,128]{2,0,1:T(8,128)S(1)} fusion(f32[256,12,128]{2,0,1:T(8,128)S(1)} %get-tuple-element.151, bf16[256,12,128]{2,0,1:T(8,128)(2,1)} %get-tuple-element.152, f32[12,256,256]{1,2,0:T(8,128)S(1)} %get-tuple-element.193, f32[12,256]{1,0:T(8,128)S(1)} %get-tuple-element.185, pred[256,256]{0,1:T(8,128)(4,1)S(1)} %and_or_fusion.1, ...), kind=kOutput, calls=%fused_computation.61 | convolution fusion | flops 206045184 | bytes 7168000 | tf_op jit(solution)/shard_map/cond/branch_1_fun/hqk,khd->qhd/dot_general | solution.py:26
  195.8 0.9 copy.67
  197.6 7.1 %all_to_all.69 = bf16[256,12,128]{2,1,0:T(8,128)(2,1)S(1)} all-to-all(bf16[256,12,128]{2,1,0:T(8,128)(2,1)S(1)} %divide_convert_fusion), channel_id=1, replica_groups=mesh['ctx'=128,'head'=2] {'head'}, dimensions={0} | all-to-all | bytes 1572864 | tf_op jit(solution)/shard_map/all_to_all | solution.py:72
  204.7 0.8 copy.55
  205.5 1.2 copy.56
  (52 shorter events, 6.4 us)
Async XLA Ops:
  0.0 6.6 %copy-start.1 = (bf16[128,3072]{1,0:T(8,128)(2,1)S(1)}, bf16[128,3072]{1,0:T(8,128)(2,1)}, u32[]{:S(2)}) copy-start(bf16[128,3072]{1,0:T(8,128)(2,1)} %param.16) | copy-start | bytes 2359300
  2.4 5.8 %all-to-all-start.1 = ((bf16[128,24,128]{0,2,1:T(8,128)(2,1)}), bf16[128,24,128]{0,2,1:T(8,128)(2,1)S(1)}, u32[]{:S(2)}, u32[]{:S(2)}) async-start(bf16[128,24,128]{0,2,1:T(8,128)(2,1)} %bitcast.17), calls=%async_computation.1 | async-start | bytes 1572864 | tf_op jit(solution)/shard_map/all_to_all | solution.py:40
  6.6 47.9 %copy-start.5 = (s32[256]{0:T(256)S(1)}, s32[256]{0:T(256)}, u32[]{:S(2)}) copy-start(s32[256]{0:T(256)} %param.18) | copy-start | bytes 3076
  6.6 50.1 %copy-start.4 = (s32[256]{0:T(256)S(1)}, s32[256]{0:T(256)}, u32[]{:S(2)}) copy-start(s32[256]{0:T(256)} %param.17) | copy-start | bytes 3076
  8.1 7.4 %all-to-all-start.2 = ((bf16[128,24,128]{0,2,1:T(8,128)(2,1)}), bf16[128,24,128]{0,2,1:T(8,128)(2,1)S(1)}, u32[]{:S(2)}, u32[]{:S(2)}) async-start(bf16[128,24,128]{0,2,1:T(8,128)(2,1)} %bitcast.23), calls=%async_computation.2 | async-start | bytes 1572864 | tf_op jit(solution)/shard_map/all_to_all | solution.py:41
  12.0 55.5 %copy-start.6 = (s32[1,4]{1,0:T(1,128)S(1)}, s32[1,4]{1,0:T(1,128)}, u32[]{:S(2)}) copy-start(s32[1,4]{1,0:T(1,128)} %param.19) | copy-start | bytes 52
  12.4 23.2 %collective-permute-start.2 = (bf16[256,12,128]{2,0,1:T(8,128)(2,1)S(1)}, bf16[256,12,128]{2,0,1:T(8,128)(2,1)}, u32[]{:S(2)}, u32[]{:S(2)}) collective-permute-start(bf16[256,12,128]{2,0,1:T(8,128)(2,1)S(1)} %bitcast.67), channel_id=1, source_target_pairs={{0,2},{2,4},{4,6},{6,8},{8,10},{10,12},{12,14},{14,16},{16,18},{18... | collective-permute-start | bytes 2359304 | tf_op jit(solution)/shard_map/ppermute | solution.py:13
  15.9 46.0 %copy-start.2 = (bf16[2,128,12,128]{3,1,0,2:T(8,128)(2,1)}, bf16[2,128,12,128]{3,1,0,2:T(8,128)(2,1)S(1)}, u32[]{:S(2)}) copy-start(bf16[2,128,12,128]{3,1,0,2:T(8,128)(2,1)S(1)} %copy.50) | copy-start | bytes 2359300
  15.9 36.6 %collective-permute-start.3 = (bf16[256,12,128]{2,0,1:T(8,128)(2,1)S(1)}, bf16[256,12,128]{2,0,1:T(8,128)(2,1)}, u32[]{:S(2)}, u32[]{:S(2)}) collective-permute-start(bf16[256,12,128]{2,0,1:T(8,128)(2,1)S(1)} %bitcast.73), channel_id=1, source_target_pairs={{0,2},{2,4},{4,6},{6,8},{8,10},{10,12},{12,14},{14,16},{16,18},{18... | collective-permute-start | bytes 2359304 | tf_op jit(solution)/shard_map/ppermute | solution.py:13
  35.7 55.1 %collective-permute-start.6 = (bf16[256,12,128]{2,0,1:T(8,128)(2,1)}, bf16[256,12,128]{2,0,1:T(8,128)(2,1)S(1)}, u32[]{:S(2)}, u32[]{:S(2)}) collective-permute-start(bf16[256,12,128]{2,0,1:T(8,128)(2,1)} %collective-permute-done.2), channel_id=1, source_target_pairs={{0,2},{2,4},{4,6},{6,8},{8,10},{10,12},{12,14},{14,16},{16,18},{18... | collective-permute-start | bytes 2359304 | tf_op jit(solution)/shard_map/ppermute | solution.py:13
  52.5 41.3 %collective-permute-start.7 = (bf16[256,12,128]{2,0,1:T(8,128)(2,1)}, bf16[256,12,128]{2,0,1:T(8,128)(2,1)}, u32[]{:S(2)}, u32[]{:S(2)}) collective-permute-start(bf16[256,12,128]{2,0,1:T(8,128)(2,1)} %collective-permute-done.3), channel_id=1, source_target_pairs={{0,2},{2,4},{4,6},{6,8},{8,10},{10,12},{12,14},{14,16},{16,18},{18... | collective-permute-start | bytes 2359304 | tf_op jit(solution)/shard_map/ppermute | solution.py:13
  54.4 31.8 %collective-permute-start.1 = (s32[256]{0:T(256)S(1)}, s32[256]{0:T(256)S(1)}, u32[]{:S(2)}, u32[]{:S(2)}) collective-permute-start(s32[256]{0:T(256)S(1)} %copy-done.5), channel_id=1, source_target_pairs={{0,2},{2,4},{4,6},{6,8},{8,10},{10,12},{12,14},{14,16},{16,18},{18... | collective-permute-start | bytes 3080 | tf_op jit(solution)/shard_map/ppermute | solution.py:13
  56.7 31.5 %collective-permute-start = (s32[256]{0:T(256)S(1)}, s32[256]{0:T(256)S(1)}, u32[]{:S(2)}, u32[]{:S(2)}) collective-permute-start(s32[256]{0:T(256)S(1)} %copy-done.4), channel_id=1, source_target_pairs={{0,2},{2,4},{4,6},{6,8},{8,10},{10,12},{12,14},{14,16},{16,18},{18... | collective-permute-start | bytes 3080 | tf_op jit(solution)/shard_map/ppermute | solution.py:13
  61.9 28.5 %all-to-all-start = ((bf16[128,24,128]{0,2,1:T(8,128)(2,1)}), bf16[128,24,128]{0,2,1:T(8,128)(2,1)S(1)}, u32[]{:S(2)}, u32[]{:S(2)}) async-start(bf16[128,24,128]{0,2,1:T(8,128)(2,1)} %bitcast.12), calls=%async_computation | async-start | bytes 1572864 | tf_op jit(solution)/shard_map/all_to_all | solution.py:39
  86.2 17.2 %collective-permute-start.5 = (s32[256]{0:T(256)S(1)}, s32[256]{0:T(256)S(1)}, u32[]{:S(2)}, u32[]{:S(2)}) collective-permute-start(s32[256]{0:T(256)S(1)} %collective-permute-done.1), channel_id=1, source_target_pairs={{0,2},{2,4},{4,6},{6,8},{8,10},{10,12},{12,14},{14,16},{16,18},{18... | collective-permute-start | bytes 3080 | tf_op jit(solution)/shard_map/ppermute | solution.py:13
  88.2 15.3 %collective-permute-start.4 = (s32[256]{0:T(256)S(1)}, s32[256]{0:T(256)S(1)}, u32[]{:S(2)}, u32[]{:S(2)}) collective-permute-start(s32[256]{0:T(256)S(1)} %collective-permute-done), channel_id=1, source_target_pairs={{0,2},{2,4},{4,6},{6,8},{8,10},{10,12},{12,14},{14,16},{16,18},{18... | collective-permute-start | bytes 3080 | tf_op jit(solution)/shard_map/ppermute | solution.py:13
  90.8 21.8 %collective-permute-start.10 = (bf16[256,12,128]{2,0,1:T(8,128)(2,1)S(1)}, bf16[256,12,128]{2,0,1:T(8,128)(2,1)}, u32[]{:S(2)}, u32[]{:S(2)}) collective-permute-start(bf16[256,12,128]{2,0,1:T(8,128)(2,1)S(1)} %collective-permute-done.6), channel_id=1, source_target_pairs={{0,2},{2,4},{4,6},{6,8},{8,10},{10,12},{12,14},{14,16},{16,18},{18... | collective-permute-start | bytes 2359304 | tf_op jit(solution)/shard_map/ppermute | solution.py:13
  93.8 35.6 %collective-permute-start.11 = (bf16[256,12,128]{2,0,1:T(8,128)(2,1)}, bf16[256,12,128]{2,0,1:T(8,128)(2,1)}, u32[]{:S(2)}, u32[]{:S(2)}) collective-permute-start(bf16[256,12,128]{2,0,1:T(8,128)(2,1)} %collective-permute-done.7), channel_id=1, source_target_pairs={{0,2},{2,4},{4,6},{6,8},{8,10},{10,12},{12,14},{14,16},{16,18},{18... | collective-permute-start | bytes 2359304 | tf_op jit(solution)/shard_map/ppermute | solution.py:13
  103.7 39.2 %copy-start.3 = (bf16[2,128,12,128]{3,1,0,2:T(8,128)(2,1)S(1)}, bf16[2,128,12,128]{3,1,0,2:T(8,128)(2,1)}, u32[]{:S(2)}) copy-start(bf16[2,128,12,128]{3,1,0,2:T(8,128)(2,1)} %copy-done.2) | copy-start | bytes 2359300
  112.6 77.2 %collective-permute-start.14 = (bf16[256,12,128]{2,0,1:T(8,128)(2,1)}, bf16[256,12,128]{2,0,1:T(8,128)(2,1)}, u32[]{:S(2)}, u32[]{:S(2)}) collective-permute-start(bf16[256,12,128]{2,0,1:T(8,128)(2,1)} %collective-permute-done.10), channel_id=1, source_target_pairs={{0,2},{2,4},{4,6},{6,8},{8,10},{10,12},{12,14},{14,16},{16,18},{18... | collective-permute-start | bytes 2359304 | tf_op jit(solution)/shard_map/ppermute | solution.py:13
  129.4 60.3 %collective-permute-start.15 = (bf16[256,12,128]{2,0,1:T(8,128)(2,1)}, bf16[256,12,128]{2,0,1:T(8,128)(2,1)}, u32[]{:S(2)}, u32[]{:S(2)}) collective-permute-start(bf16[256,12,128]{2,0,1:T(8,128)(2,1)} %collective-permute-done.11), channel_id=1, source_target_pairs={{0,2},{2,4},{4,6},{6,8},{8,10},{10,12},{12,14},{14,16},{16,18},{18... | collective-permute-start | bytes 2359304 | tf_op jit(solution)/shard_map/ppermute | solution.py:13
  136.6 26.6 %collective-permute-start.8 = (s32[256]{0:T(256)S(1)}, s32[256]{0:T(256)}, u32[]{:S(2)}, u32[]{:S(2)}) collective-permute-start(s32[256]{0:T(256)S(1)} %collective-permute-done.4), channel_id=1, source_target_pairs={{0,2},{2,4},{4,6},{6,8},{8,10},{10,12},{12,14},{14,16},{16,18},{18... | collective-permute-start | bytes 3080 | tf_op jit(solution)/shard_map/ppermute | solution.py:13
  140.7 28.8 %collective-permute-start.9 = (s32[256]{0:T(256)S(1)}, s32[256]{0:T(256)}, u32[]{:S(2)}, u32[]{:S(2)}) collective-permute-start(s32[256]{0:T(256)S(1)} %collective-permute-done.5), channel_id=1, source_target_pairs={{0,2},{2,4},{4,6},{6,8},{8,10},{10,12},{12,14},{14,16},{16,18},{18... | collective-permute-start | bytes 3080 | tf_op jit(solution)/shard_map/ppermute | solution.py:13
  163.1 26.6 %collective-permute-start.12 = (s32[256]{0:T(256)}, s32[256]{0:T(256)S(1)}, u32[]{:S(2)}, u32[]{:S(2)}) collective-permute-start(s32[256]{0:T(256)} %collective-permute-done.8), channel_id=1, source_target_pairs={{0,2},{2,4},{4,6},{6,8},{8,10},{10,12},{12,14},{14,16},{16,18},{18... | collective-permute-start | bytes 3080 | tf_op jit(solution)/shard_map/ppermute | solution.py:13
  169.5 20.2 %collective-permute-start.13 = (s32[256]{0:T(256)}, s32[256]{0:T(256)S(1)}, u32[]{:S(2)}, u32[]{:S(2)}) collective-permute-start(s32[256]{0:T(256)} %collective-permute-done.9), channel_id=1, source_target_pairs={{0,2},{2,4},{4,6},{6,8},{8,10},{10,12},{12,14},{14,16},{16,18},{18... | collective-permute-start | bytes 3080 | tf_op jit(solution)/shard_map/ppermute | solution.py:13
where the time goes:
time: 208 us; the launch traced here: 207 us
  waiting for transfers between devices  83.7 us (40%)
  starting transfers between devices  75 us (36%)
  matrix products  18.1 us (9%)
  local copies, waits for them, and re-layouts  10.8 us (5%)
  blocking collectives  7.13 us (3%)
  other arithmetic  5.9 us (3%)
  between operations  4.37 us (2%)
    ppermute x16, waiting for transfers between devices, passed_along(): lax.ppermute(value, axis, [(source, source + steps) for source in range(i...  83.3 us
    ppermute x16, starting transfers between devices, passed_along(): lax.ppermute(value, axis, [(source, source + steps) for source in range(i...  61.3 us
    dot_general x5, matrix products, attend_block(): jnp.einsum('hqk,khd->qhd', weights.astype(jnp.bfloat16), value_rows, pref...  11.6 us
    all_to_all x1, blocking collectives, shards(): lax.all_to_all(result, 'head', split_axis=0, concat_axis=1, tiled=True)  7.13 us
    dot_general x5, matrix products, attend_block(): jnp.einsum('qhd,khd->hqk', query_rows, key_rows, preferred_element_type=j...  6.48 us
    unnamed x15, local copies, waits for them, and re-layouts  5.86 us
    all_to_all x1, starting transfers between devices, shards(): lax.all_to_all(query_in, 'head', split_axis=1, concat_axis=0, tiled=True)  5.6 us
    all_to_all x1, starting transfers between devices, shards(): lax.all_to_all(key_in, 'head', split_axis=1, concat_axis=0, tiled=True)  4.2 us
  transfers between devices with their start and end apart: 19, of which 7 were waited for; matrix products, arithmetic and copies ran while one was open for 11% of the time, Pallas kernels for 0%

commit v1 on v0

v1 whole, which is shorter than its diff:
```python
import jax
import jax.numpy as jnp
from jax import lax
from jax.experimental import pallas as pl
from jax.experimental.pallas import tpu as pltpu
from jax.sharding import PartitionSpec as P

HD = 128
WIN = 4
BLK = 256
SHARE = 128
ROW = 4
TEAM = 2 * ROW
HEADS = 3
SPAN = ROW * BLK
WINDOW = (WIN + 1) * BLK
MESH = pl.DeviceIdType.MESH
LOG2E = 1.4426950408889634
MASKED = -1e30


def kernel(q_ref, k_ref, v_ref, clip_ref, group_ref, kinds_ref, o_ref,
           mine, table, kv, qb, ob, bias,
           id_send, id_recv, idf_send, idf_recv, x_send, x_recv, q_send, q_recv, y_send, y_recv, o_send, o_recv):
    ctx = lax.axis_index("ctx")
    core = lax.axis_index("head")
    x = ctx % ROW
    me = 2 * x + core
    base = ctx - x
    has_next = ctx < 128 - ROW
    has_prev = ctx >= ROW

    def device(place):
        return (base + place // 2, place % 2)

    after, before = (ctx + ROW, core), (ctx - ROW, core)
    partners = [(me + step) % TEAM for step in (2, 6, 4, 3, 7, 5, 1)]

    barrier = pltpu.get_barrier_semaphore()
    for place in partners:
        pl.semaphore_signal(barrier, inc=1, device_id=device(place), device_id_type=MESH)

    @pl.when(has_next)
    def _():
        pl.semaphore_signal(barrier, inc=1, device_id=after, device_id_type=MESH)

    @pl.when(has_prev)
    def _():
        pl.semaphore_signal(barrier, inc=1, device_id=before, device_id_type=MESH)

    mine[0:1] = clip_ref[...]
    mine[1:2] = group_ref[...]
    for d in range(WIN):
        mine[2 + d:3 + d] = jnp.full((1, BLK), kinds_ref[0, d], jnp.int32)
    mine[6:8] = jnp.zeros((2, BLK), jnp.int32)

    @pl.when(jnp.logical_not(has_prev))
    def _():
        kv[:, :, 0:SPAN, :] = jnp.zeros((2, HEADS, SPAN, HD), jnp.bfloat16)
        table[0:ROW] = jnp.zeros((ROW, 8, BLK), jnp.int32)

    pl.semaphore_wait(barrier, TEAM - 1 + jnp.where(has_next, 1, 0) + jnp.where(has_prev, 1, 0))

    id_copies = []
    for n, step in enumerate((2, 6, 4)):
        id_copies.append(pltpu.make_async_remote_copy(
            mine, table.at[ROW + x], id_send.at[n], id_recv.at[n],
            device_id=device((me + step) % TEAM), device_id_type=MESH))
        id_copies[-1].start()
    own_ids = pltpu.make_async_copy(mine, table.at[ROW + x], id_recv.at[3])
    own_ids.start()

    def share(ref, h, landing, send, recv):
        def columns(place):
            return pl.ds(pl.multiple_of(HD * (HEADS * place + h), HD), HD)

        rows = pl.ds(pl.multiple_of(SHARE * me, SHARE), SHARE)
        for place in partners:
            pltpu.make_async_remote_copy(
                ref.at[:, columns(place)], landing.at[rows], send, recv,
                device_id=device(place), device_id_type=MESH).start()
        pltpu.make_async_copy(ref.at[:, columns(me)], landing.at[rows], recv).start()

    own = pl.ds(SPAN, SPAN)
    for h in range(HEADS):
        share(k_ref, h, kv.at[0, h, own], x_send.at[0, h], x_recv.at[0, h])
        share(v_ref, h, kv.at[1, h, own], x_send.at[1, h], x_recv.at[1, h])
        share(q_ref, h, qb.at[h], q_send.at[h], q_recv.at[h])

    def await_bytes(ref, sem):
        pltpu.make_async_copy(ref, ref, sem).wait()

    def forward(t, h):
        return pltpu.make_async_remote_copy(
            kv.at[t, h, own], kv.at[t, h, pl.ds(0, SPAN)], y_send.at[t, h], y_recv.at[t, h],
            device_id=after, device_id_type=MESH)

    def pass_on(h):
        for t in range(2):
            await_bytes(kv.at[t, h, own], x_recv.at[t, h])

            @pl.when(has_next)
            def _():
                forward(t, h).start()

    def table_forward():
        return pltpu.make_async_remote_copy(
            table.at[pl.ds(ROW, ROW)], table.at[pl.ds(0, ROW)], idf_send, idf_recv,
            device_id=after, device_id_type=MESH)

    for copy in id_copies:
        copy.wait()
    own_ids.wait()

    @pl.when(has_next)
    def _():
        table_forward().start()

    pass_on(0)

    @pl.when(has_prev)
    def _():
        table_forward().wait_recv()

    def build(i, carry):
        about = table[ROW + i]
        column = jnp.transpose(about.astype(jnp.float32))
        query_clip, query_group = column[:, 0:1], column[:, 1:2]
        for w in range(WIN + 1):
            there = table[i + w].astype(jnp.float32)
            allowed = (there[0:1] == query_clip) & (there[1:2] <= query_group)
            if w < WIN:
                kind = about[2 + WIN - 1 - w:3 + WIN - 1 - w]
                kind = jnp.where(has_prev | (i + w >= ROW), kind, 0)
                allowed = (kind == 2) | ((kind == 1) & allowed)
            bias[i, :, w * BLK:(w + 1) * BLK] = jnp.where(allowed, 0.0, MASKED)
        return carry

    lax.fori_loop(0, ROW, build, 0)

    def attend(h):
        def block(i, carry):
            start = pl.multiple_of(i * BLK, BLK)
            rows = qb[h, pl.ds(start, BLK)]
            keys = kv[0, h, pl.ds(start, WINDOW)]
            scores = lax.dot_general(rows, keys, (((1,), (1,)), ((), ())), preferred_element_type=jnp.float32)
            scores = scores + bias[i]
            highest = jnp.max(scores, axis=1, keepdims=True)
            weights = jnp.exp2((scores - highest) * (LOG2E * HD ** -0.5))
            total = jnp.sum(weights, axis=1, keepdims=True)
            out = jnp.dot(weights.astype(jnp.bfloat16), kv[1, h, pl.ds(start, WINDOW)], preferred_element_type=jnp.float32)
            ob[h, pl.ds(start, BLK)] = (out / total).astype(jnp.bfloat16)
            return carry

        lax.fori_loop(0, ROW, block, 0)

    def give_back(h):
        columns = pl.ds(pl.multiple_of(HD * (HEADS * me + h), HD), HD)
        for place in partners:
            pltpu.make_async_remote_copy(
                ob.at[h, pl.ds(pl.multiple_of(SHARE * place, SHARE), SHARE)], o_ref.at[:, columns],
                o_send.at[h], o_recv.at[h], device_id=device(place), device_id_type=MESH).start()
        pltpu.make_async_copy(
            ob.at[h, pl.ds(pl.multiple_of(SHARE * me, SHARE), SHARE)], o_ref.at[:, columns], o_recv.at[h]).start()

    for h in range(HEADS):
        if h + 1 < HEADS:
            pass_on(h + 1)
        await_bytes(qb.at[h], q_recv.at[h])

        @pl.when(has_prev)
        def _():
            forward(0, h).wait_recv()
            forward(1, h).wait_recv()

        attend(h)
        give_back(h)

    sent = (TEAM - 1) * SHARE
    for h in range(HEADS):
        for t in range(2):
            await_bytes(kv.at[t, h, pl.ds(0, sent)], x_send.at[t, h])

            @pl.when(has_next)
            def _():
                forward(t, h).wait_send()

        await_bytes(qb.at[h, pl.ds(0, sent)], q_send.at[h])

    @pl.when(has_next)
    def _():
        table_forward().wait_send()

    for h in range(HEADS):
        await_bytes(qb.at[h, pl.ds(0, sent)], o_send.at[h])
        await_bytes(qb.at[h], o_recv.at[h])


def shards(queries, keys, values, clip_ids, group_ids, pair_kinds):
    hbm = pl.BlockSpec(memory_space=pl.ANY)
    vmem = pl.BlockSpec(memory_space=pltpu.VMEM)
    dma = pltpu.SemaphoreType.DMA
    return pl.pallas_call(
        kernel,
        out_shape=jax.ShapeDtypeStruct(queries.shape, jnp.bfloat16),
        in_specs=[hbm, hbm, hbm, vmem, vmem, pl.BlockSpec(memory_space=pltpu.SMEM)],
        out_specs=hbm,
        scratch_shapes=[
            pltpu.VMEM((8, BLK), jnp.int32),
            pltpu.VMEM((2 * ROW, 8, BLK), jnp.int32),
            pltpu.VMEM((2, HEADS, 2 * SPAN, HD), jnp.bfloat16),
            pltpu.VMEM((HEADS, SPAN, HD), jnp.bfloat16),
            pltpu.VMEM((HEADS, SPAN, HD), jnp.bfloat16),
            pltpu.VMEM((ROW, BLK, WINDOW), jnp.float32),
            dma((3,)), dma((4,)), dma, dma,
            dma((2, HEADS)), dma((2, HEADS)), dma((HEADS,)), dma((HEADS,)),
            dma((2, HEADS)), dma((2, HEADS)), dma((HEADS,)), dma((HEADS,)),
        ],
        compiler_params=pltpu.CompilerParams(
            collective_id=0, has_side_effects=True, vmem_limit_bytes=60 * 1024 * 1024),
    )(queries, keys, values, clip_ids.reshape(1, BLK), group_ids.reshape(1, BLK), pair_kinds)


def solution(mesh):
    tokens = P(("ctx", "head"), None)
    return jax.shard_map(
        shards, mesh=mesh, in_specs=(tokens, tokens, tokens, P("ctx"), P("ctx"), P("ctx", None)),
        out_specs=tokens, check_vma=False)
```

time: 208 us -> 59.2 us (0.28)
  the two profiles are of different devices: /device:TPU:121 before, /device:TPU:161 now
where the time goes in v1:
time: 59.2 us; the launch traced here: 59.1 us
  Pallas kernels  57 us (96%)
  local copies, waits for them, and re-layouts  2.06 us (3%)
    pallas_call x1, Pallas kernels, shards(): pl.pallas_call(kernel, out_shape=jax.ShapeDtypeStruct(queries.shape, jnp....  57 us
    unnamed x1, local copies, waits for them, and re-layouts  2.06 us

profile of v1, /device:TPU:161, one launch (start us, length us, event | category | flops | bytes accessed | tf_op | source)
XLA Modules:
  0.0 59.1 jit_solution(3819641605486007106)
XLA Ops:
  0.0 57.0 %shard_map.64 = bf16[128,3072]{1,0:T(8,128)(2,1)} custom-call(bf16[128,3072]{1,0:T(8,128)(2,1)} %q_ref.1, bf16[128,3072]{1,0:T(8,128)(2,1)} %k_ref.1, bf16[128,3072]{1,0:T(8,128)(2,1)} %v_ref.1, s32[1,256]{1,0:T(1,128)} %bitcast.2, s32[1,256]{1,0:T(1,128)} %bitcast.3, s32[1,4]{1,0:T(1,128)} %kinds_ref.1), custom_call_target="tpu_custom_call" | custom-call | tf_op jit(solution)/shard_map/pallas_call | solution.py:203
  57.0 2.1 %copy.8 = bf16[128,3072]{1,0:T(8,128)(2,1)} copy(bf16[128,3072]{1,0:T(8,128)(2,1)} %shard_map.64) | data formatting | bytes 1572864

commit v2 on v1

v2 whole, which is shorter than its diff:
```python
import jax
import jax.numpy as jnp
from jax import lax
from jax.experimental import pallas as pl
from jax.experimental.pallas import tpu as pltpu
from jax.sharding import PartitionSpec as P

HD = 128
WIN = 4
BLK = 256
SHARE = 128
ROW = 4
TEAM = 2 * ROW
HEADS = 3
SPAN = ROW * BLK
WINDOW = (WIN + 1) * BLK
BACK = 2
BACKED = BACK * BLK
MESH = pl.DeviceIdType.MESH
FACTOR = 1.4426950408889634 * HD ** -0.5
MASKED = -1e30


def kernel(q_ref, k_ref, v_ref, clip_ref, group_ref, kinds_ref, o_ref,
           mine, table, kv, qb, ob, qn, on, sn, op, sp, bias_a, bias_b, bias_n,
           tops, totals, outs, weights_a, weights_b,
           id_send, id_recv, idf_send, idf_recv, idb_send, idb_recv, x_send, x_recv, q_send, q_recv, y_send, y_recv,
           qb_send, qb_recv, p_send, p_recv, s_send, s_recv, o_send, o_recv):
    ctx = lax.axis_index("ctx")
    core = lax.axis_index("head")
    x = ctx % ROW
    me = 2 * x + core
    base = ctx - x
    has_next = ctx < 128 - ROW
    has_prev = ctx >= ROW

    def device(place):
        return (base + place // 2, place % 2)

    after, before = (ctx + ROW, core), (ctx - ROW, core)
    partners = [(me + step) % TEAM for step in (2, 6, 4, 3, 7, 5, 1)]

    barrier = pltpu.get_barrier_semaphore()
    for place in partners:
        pl.semaphore_signal(barrier, inc=1, device_id=device(place), device_id_type=MESH)

    @pl.when(has_next)
    def _():
        pl.semaphore_signal(barrier, inc=1, device_id=after, device_id_type=MESH)

    @pl.when(has_prev)
    def _():
        pl.semaphore_signal(barrier, inc=1, device_id=before, device_id_type=MESH)

    mine[0:1] = clip_ref[...]
    mine[1:2] = group_ref[...]
    for d in range(WIN):
        mine[2 + d:3 + d] = jnp.full((1, BLK), kinds_ref[0, d], jnp.int32)
    mine[6:8] = jnp.zeros((2, BLK), jnp.int32)

    @pl.when(jnp.logical_not(has_prev))
    def _():
        kv[:, :, BACKED:SPAN, :] = jnp.zeros((2, HEADS, SPAN - BACKED, HD), jnp.bfloat16)
        table[0:ROW] = jnp.zeros((ROW, 8, BLK), jnp.int32)
        op[...] = jnp.zeros((HEADS, BACKED, HD), jnp.bfloat16)
        sp[...] = jnp.full((HEADS, BACK, 8, BLK), MASKED, jnp.float32)

    pl.semaphore_wait(barrier, TEAM - 1 + jnp.where(has_next, 1, 0) + jnp.where(has_prev, 1, 0))

    id_copies = []
    for n, step in enumerate((2, 6, 4)):
        id_copies.append(pltpu.make_async_remote_copy(
            mine, table.at[ROW + x], id_send.at[n], id_recv.at[n],
            device_id=device((me + step) % TEAM), device_id_type=MESH))
        id_copies[-1].start()
    own_ids = pltpu.make_async_copy(mine, table.at[ROW + x], id_recv.at[3])
    own_ids.start()

    def share(ref, h, landing, send, recv):
        def columns(place):
            return pl.ds(pl.multiple_of(HD * (HEADS * place + h), HD), HD)

        rows = pl.ds(pl.multiple_of(SHARE * me, SHARE), SHARE)
        for place in partners:
            pltpu.make_async_remote_copy(
                ref.at[:, columns(place)], landing.at[rows], send, recv,
                device_id=device(place), device_id_type=MESH).start()
        pltpu.make_async_copy(ref.at[:, columns(me)], landing.at[rows], recv).start()

    own = pl.ds(SPAN, SPAN)

    def share_key(h):
        share(k_ref, h, kv.at[0, h, own], x_send.at[0, h], x_recv.at[0, h])

    def share_value(h):
        share(v_ref, h, kv.at[1, h, own], x_send.at[1, h], x_recv.at[1, h])

    def share_query(h, part):
        @pl.when(x // BACK == part)
        def _():
            share(q_ref, h, qb.at[h], q_send.at[h], q_recv.at[part, h])

    for h in range(HEADS):
        share_query(h, 0)
        share_key(h)
        share_value(h)
    for h in range(HEADS):
        share_query(h, 1)

    def await_bytes(ref, sem):
        pltpu.make_async_copy(ref, ref, sem).wait()

    def remote(src, dst, send, recv, to):
        return pltpu.make_async_remote_copy(src, dst, send, recv, device_id=to, device_id_type=MESH)

    def forward(t, h):
        return remote(kv.at[t, h, pl.ds(SPAN + BACKED, SPAN - BACKED)], kv.at[t, h, pl.ds(BACKED, SPAN - BACKED)],
                      y_send.at[t, h], y_recv.at[t, h], after)

    def backward(h):
        return remote(qb.at[h, pl.ds(0, BACKED)], qn.at[h], qb_send.at[h], qb_recv.at[h], before)

    def partial_out(h):
        return remote(on.at[h], op.at[h], p_send.at[h], p_recv.at[h], after)

    def partial_stats(h):
        return remote(sn.at[h], sp.at[h], s_send.at[h], s_recv.at[h], after)

    def table_forward():
        return remote(table.at[pl.ds(ROW, ROW)], table.at[pl.ds(0, ROW)], idf_send, idf_recv, after)

    def table_backward():
        return remote(table.at[pl.ds(ROW, ROW)], table.at[pl.ds(2 * ROW, ROW)], idb_send, idb_recv, before)

    def when(condition, *actions):
        @pl.when(condition)
        def _():
            for action in actions:
                action()

    def pass_on(t, h):
        await_bytes(kv.at[t, h, own], x_recv.at[t, h])
        when(has_next, lambda: forward(t, h).start())

    def pass_back(h):
        await_bytes(qb.at[h, pl.ds(0, BACKED)], q_recv.at[0, h])
        when(has_prev, lambda: backward(h).start())

    for copy in id_copies:
        copy.wait()
    own_ids.wait()
    when(has_next, lambda: table_forward().start())
    when(has_prev, lambda: table_backward().start())

    def pair(query_slot, key_slot):
        d = query_slot - key_slot
        if d < 0 or d > WIN:
            return jnp.full((BLK, BLK), MASKED, jnp.float32)
        about = table[query_slot]
        column = jnp.transpose(about.astype(jnp.float32))
        there = table[key_slot].astype(jnp.float32)
        allowed = (there[0:1] == column[:, 0:1]) & (there[1:2] <= column[:, 1:2])
        if d:
            kind = about[1 + d:2 + d]
            if key_slot < ROW:
                kind = jnp.where(has_prev, kind, 0)
            allowed = (kind == 2) | ((kind == 1) & allowed)
        return jnp.where(allowed, 0.0, MASKED)

    def terms(ref, i, query_slot, slots):
        for n, slot in enumerate(slots):
            ref[i, :, n * BLK:(n + 1) * BLK] = pair(query_slot, slot)

    def weigh(queries, keys, term):
        scores = lax.dot_general(queries, keys, (((1,), (1,)), ((), ())), preferred_element_type=jnp.float32)
        scores = scores + term
        highest = jnp.max(scores, axis=1, keepdims=True)
        weights = jnp.exp2((scores - highest) * FACTOR)
        return highest, jnp.sum(weights, axis=1, keepdims=True), weights.astype(jnp.bfloat16)

    def blend(weights, values):
        return jnp.dot(weights, values, preferred_element_type=jnp.float32)

    def block(i):
        return pl.ds(pl.multiple_of(i * BLK, BLK), BLK)

    def loop(body):
        def step(i, carry):
            body(i)
            return carry

        lax.fori_loop(0, BACK, step, 0)

    near = pl.ds(SPAN, BACKED)
    front = pl.ds(BACKED, SPAN)

    def partial(h):
        def body(i):
            highest, total, weights = weigh(qn[h, block(i)], kv[0, h, near], bias_n[i])
            on[h, block(i)] = blend(weights, kv[1, h, near]).astype(jnp.bfloat16)
            lane = lax.broadcasted_iota(jnp.int32, (BLK, HD), 1)
            sn[h, i] = jnp.transpose(jnp.where(lane == 0, highest, total))[0:8]

        loop(body)
        partial_out(h).start()
        partial_stats(h).start()

    def give_back(h, i):
        columns = pl.ds(pl.multiple_of(HD * (HEADS * me + h), HD), HD)
        for place in (2 * i, 2 * i + 1):
            rows = ob.at[h, pl.ds(pl.multiple_of(SHARE * place, SHARE), SHARE)]

            @pl.when(me != place)
            def _():
                remote(rows, o_ref.at[:, columns], o_send.at[h], o_recv.at[h], device(place)).start()

            @pl.when(me == place)
            def _():
                pltpu.make_async_copy(rows, o_ref.at[:, columns], o_recv.at[h]).start()

    def weigh_first(h):
        def body(i):
            tops[i], totals[i], weights_a[i] = weigh(qb[h, block(i)], kv[0, h, front], bias_a[i])

        loop(body)

    def blend_first(h):
        def body(i):
            outs[i] = blend(weights_a[i], kv[1, h, front])

        loop(body)

    def merge(h):
        def body(i):
            stats = jnp.transpose(sp[h, i])
            highest, other = tops[i], stats[:, 0:1]
            top = jnp.maximum(highest, other)
            here, there = jnp.exp2((highest - top) * FACTOR), jnp.exp2((other - top) * FACTOR)
            total = totals[i] * here + stats[:, 1:2] * there
            out = outs[i] * here + op[h, block(i)].astype(jnp.float32) * there
            ob[h, block(i)] = (out / total).astype(jnp.bfloat16)
            give_back(h, i)

        loop(body)

    def weigh_last(h):
        def body(i):
            _, totals[BACK + i], weights_b[i] = weigh(
                qb[h, block(BACK + i)], kv[0, h, pl.ds(pl.multiple_of((BACK + i) * BLK, BLK), WINDOW)], bias_b[i])

        loop(body)

    def blend_last(h):
        def body(i):
            out = blend(weights_b[i], kv[1, h, pl.ds(pl.multiple_of((BACK + i) * BLK, BLK), WINDOW)])
            ob[h, block(BACK + i)] = (out / totals[BACK + i]).astype(jnp.bfloat16)
            give_back(h, BACK + i)

        loop(body)

    def await_keys(h):
        when(has_prev, lambda: forward(0, h).wait_recv())

    def await_values(h):
        when(has_prev, lambda: forward(1, h).wait_recv())

    def await_last(h):
        await_bytes(qb.at[h, pl.ds(BACKED, SPAN - BACKED)], q_recv.at[1, h])

    def await_partial(h):
        when(has_prev, lambda: partial_out(h).wait_recv(), lambda: partial_stats(h).wait_recv())

    def next_part(h):
        @pl.when(has_next)
        def _():
            backward(h).wait_recv()
            partial(h)

    pass_back(0)
    pass_on(0, 0)
    when(has_next, lambda: table_backward().wait_recv())

    @pl.when(has_next)
    def _():
        for i in range(BACK):
            terms(bias_n, i, 2 * ROW + i, range(ROW, ROW + BACK))

    pass_on(1, 0)
    next_part(0)
    pass_back(1)
    when(has_prev, lambda: table_forward().wait_recv())
    for i in range(BACK):
        terms(bias_a, i, ROW + i, range(BACK, BACK + ROW))
    pass_on(0, 1)
    await_keys(0)
    weigh_first(0)
    await_values(0)
    blend_first(0)
    pass_on(1, 1)
    next_part(1)
    pass_back(2)
    await_partial(0)
    merge(0)
    for i in range(BACK):
        terms(bias_b, i, ROW + BACK + i, range(BACK + i, BACK + i + WIN + 1))
    pass_on(0, 2)
    await_keys(1)
    weigh_first(1)
    pass_on(1, 2)
    next_part(2)
    await_values(1)
    blend_first(1)
    await_last(0)
    weigh_last(0)
    blend_last(0)
    await_partial(1)
    merge(1)
    await_last(1)
    weigh_last(1)
    blend_last(1)
    await_keys(2)
    weigh_first(2)
    await_last(2)
    weigh_last(2)
    await_values(2)
    blend_first(2)
    blend_last(2)
    await_partial(2)
    merge(2)

    sent = (TEAM - 1) * SHARE
    for h in range(HEADS):
        for t in range(2):
            await_bytes(kv.at[t, h, pl.ds(0, sent)], x_send.at[t, h])
        await_bytes(qb.at[h, pl.ds(0, sent)], q_send.at[h])

    @pl.when(has_next)
    def _():
        table_forward().wait_send()
        for h in range(HEADS):
            forward(0, h).wait_send()
            forward(1, h).wait_send()
            partial_out(h).wait_send()
            partial_stats(h).wait_send()

    @pl.when(has_prev)
    def _():
        table_backward().wait_send()
        for h in range(HEADS):
            backward(h).wait_send()

    for h in range(HEADS):
        await_bytes(qb.at[h, pl.ds(0, sent)], o_send.at[h])
        await_bytes(qb.at[h], o_recv.at[h])


def shards(queries, keys, values, clip_ids, group_ids, pair_kinds):
    hbm = pl.BlockSpec(memory_space=pl.ANY)
    vmem = pl.BlockSpec(memory_space=pltpu.VMEM)
    dma = pltpu.SemaphoreType.DMA
    bf16 = jnp.bfloat16
    return pl.pallas_call(
        kernel,
        out_shape=jax.ShapeDtypeStruct(queries.shape, bf16),
        in_specs=[hbm, hbm, hbm, vmem, vmem, pl.BlockSpec(memory_space=pltpu.SMEM)],
        out_specs=hbm,
        scratch_shapes=[
            pltpu.VMEM((8, BLK), jnp.int32),
            pltpu.VMEM((3 * ROW, 8, BLK), jnp.int32),
            pltpu.VMEM((2, HEADS, 2 * SPAN, HD), bf16),
            pltpu.VMEM((HEADS, SPAN, HD), bf16),
            pltpu.VMEM((HEADS, SPAN, HD), bf16),
            pltpu.VMEM((HEADS, BACKED, HD), bf16),
            pltpu.VMEM((HEADS, BACKED, HD), bf16),
            pltpu.VMEM((HEADS, BACK, 8, BLK), jnp.float32),
            pltpu.VMEM((HEADS, BACKED, HD), bf16),
            pltpu.VMEM((HEADS, BACK, 8, BLK), jnp.float32),
            pltpu.VMEM((BACK, BLK, SPAN), jnp.float32),
            pltpu.VMEM((BACK, BLK, WINDOW), jnp.float32),
            pltpu.VMEM((BACK, BLK, BACKED), jnp.float32),
            pltpu.VMEM((BACK, BLK, 1), jnp.float32),
            pltpu.VMEM((ROW, BLK, 1), jnp.float32),
            pltpu.VMEM((BACK, BLK, HD), jnp.float32),
            pltpu.VMEM((BACK, BLK, SPAN), bf16),
            pltpu.VMEM((BACK, BLK, WINDOW), bf16),
            dma((3,)), dma((4,)), dma, dma, dma, dma,
            dma((2, HEADS)), dma((2, HEADS)), dma((HEADS,)), dma((2, HEADS)),
            dma((2, HEADS)), dma((2, HEADS)), dma((HEADS,)), dma((HEADS,)),
            dma((HEADS,)), dma((HEADS,)), dma((HEADS,)), dma((HEADS,)), dma((HEADS,)), dma((HEADS,)),
        ],
        compiler_params=pltpu.CompilerParams(
            collective_id=0, has_side_effects=True, vmem_limit_bytes=60 * 1024 * 1024),
    )(queries, keys, values, clip_ids.reshape(1, BLK), group_ids.reshape(1, BLK), pair_kinds)


def solution(mesh):
    tokens = P(("ctx", "head"), None)
    return jax.shard_map(
        shards, mesh=mesh, in_specs=(tokens, tokens, tokens, P("ctx"), P("ctx"), P("ctx", None)),
        out_specs=tokens, check_vma=False)
```

time: 59.2 us -> 52.3 us (0.88)
  Pallas kernels: 57 us -> 50.1 us
    pallas_call x1, Pallas kernels: 57 us -> 50.1 us  [shards(): pl.pallas_call(kernel, out_shape=jax.ShapeDtypeStruct(queries.shape, bf16...]
where the time goes in v2:
time: 52.3 us; the launch traced here: 52.2 us
  Pallas kernels  50.1 us (96%)
  local copies, waits for them, and re-layouts  2.06 us (4%)
    pallas_call x1, Pallas kernels, shards(): pl.pallas_call(kernel, out_shape=jax.ShapeDtypeStruct(queries.shape, bf16...  50.1 us
    unnamed x1, local copies, waits for them, and re-layouts  2.06 us

profile of v2, /device:TPU:161, one launch (start us, length us, event | category | flops | bytes accessed | tf_op | source)
XLA Modules:
  0.0 52.2 jit_solution(7576679345726734181)
XLA Ops:
  0.0 50.1 %shard_map.64 = bf16[128,3072]{1,0:T(8,128)(2,1)} custom-call(bf16[128,3072]{1,0:T(8,128)(2,1)} %q_ref.1, bf16[128,3072]{1,0:T(8,128)(2,1)} %k_ref.1, bf16[128,3072]{1,0:T(8,128)(2,1)} %v_ref.1, s32[1,256]{1,0:T(1,128)} %bitcast.2, s32[1,256]{1,0:T(1,128)} %bitcast.3, s32[1,4]{1,0:T(1,128)} %kinds_ref.1), custom_call_target="tpu_custom_call" | custom-call | tf_op jit(solution)/shard_map/pallas_call | solution.py:362
  50.1 2.1 %copy.8 = bf16[128,3072]{1,0:T(8,128)(2,1)} copy(bf16[128,3072]{1,0:T(8,128)(2,1)} %shard_map.64) | data formatting | bytes 1572864

commit v3 on v2

--- a/solution.py
+++ b/solution.py
@@ -14,15 +14,16 @@
 HEADS = 3
 SPAN = ROW * BLK
 WINDOW = (WIN + 1) * BLK
-BACK = 2
-BACKED = BACK * BLK
+BACK = (0, 3, 3)
+MOST = max(BACK)
+SPLIT = tuple(h for h in range(HEADS) if BACK[h])
 MESH = pl.DeviceIdType.MESH
 FACTOR = 1.4426950408889634 * HD ** -0.5
 MASKED = -1e30
 
 
 def kernel(q_ref, k_ref, v_ref, clip_ref, group_ref, kinds_ref, o_ref,
-           mine, table, kv, qb, ob, qn, on, sn, op, sp, bias_a, bias_b, bias_n,
+           mine, table, kv, qb, ob, qn, on, sn, op, sp, bias, bias_n,
            tops, totals, outs, weights_a, weights_b,
            id_send, id_recv, idf_send, idf_recv, idb_send, idb_recv, x_send, x_recv, q_send, q_recv, y_send, y_recv,
            qb_send, qb_recv, p_send, p_recv, s_send, s_recv, o_send, o_recv):
@@ -60,10 +61,10 @@
 
     @pl.when(jnp.logical_not(has_prev))
     def _():
-        kv[:, :, BACKED:SPAN, :] = jnp.zeros((2, HEADS, SPAN - BACKED, HD), jnp.bfloat16)
+        kv[:, :, 0:SPAN, :] = jnp.zeros((2, HEADS, SPAN, HD), jnp.bfloat16)
         table[0:ROW] = jnp.zeros((ROW, 8, BLK), jnp.int32)
-        op[...] = jnp.zeros((HEADS, BACKED, HD), jnp.bfloat16)
-        sp[...] = jnp.full((HEADS, BACK, 8, BLK), MASKED, jnp.float32)
+        op[...] = jnp.zeros((HEADS, MOST * BLK, HD), jnp.bfloat16)
+        sp[...] = jnp.full((HEADS, MOST, 8, BLK), MASKED, jnp.float32)
 
     pl.semaphore_wait(barrier, TEAM - 1 + jnp.where(has_next, 1, 0) + jnp.where(has_prev, 1, 0))
 
@@ -95,17 +96,16 @@
     def share_value(h):
         share(v_ref, h, kv.at[1, h, own], x_send.at[1, h], x_recv.at[1, h])
 
-    def share_query(h, part):
-        @pl.when(x // BACK == part)
-        def _():
-            share(q_ref, h, qb.at[h], q_send.at[h], q_recv.at[part, h])
-
-    for h in range(HEADS):
-        share_query(h, 0)
+    def share_query(h):
+        share(q_ref, h, qb.at[h], q_send.at[h], q_recv.at[h])
+
+    share_key(0)
+    share_value(0)
+    for h in SPLIT:
+        share_query(h)
         share_key(h)
         share_value(h)
-    for h in range(HEADS):
-        share_query(h, 1)
+    share_query(0)
 
     def await_bytes(ref, sem):
         pltpu.make_async_copy(ref, ref, sem).wait()
@@ -114,17 +114,20 @@
         return pltpu.make_async_remote_copy(src, dst, send, recv, device_id=to, device_id_type=MESH)
 
     def forward(t, h):
-        return remote(kv.at[t, h, pl.ds(SPAN + BACKED, SPAN - BACKED)], kv.at[t, h, pl.ds(BACKED, SPAN - BACKED)],
+        first = BACK[h] * BLK
+        return remote(kv.at[t, h, pl.ds(SPAN + first, SPAN - first)], kv.at[t, h, pl.ds(first, SPAN - first)],
                       y_send.at[t, h], y_recv.at[t, h], after)
 
     def backward(h):
-        return remote(qb.at[h, pl.ds(0, BACKED)], qn.at[h], qb_send.at[h], qb_recv.at[h], before)
-
-    def partial_out(h):
-        return remote(on.at[h], op.at[h], p_send.at[h], p_recv.at[h], after)
-
-    def partial_stats(h):
-        return remote(sn.at[h], sp.at[h], s_send.at[h], s_recv.at[h], after)
+        first = pl.ds(0, BACK[h] * BLK)
+        return remote(qb.at[h, first], qn.at[h, first], qb_send.at[h], qb_recv.at[h], before)
+
+    def partial_out(h, i):
+        return remote(on.at[h, pl.ds(i * BLK, BLK)], op.at[h, pl.ds(i * BLK, BLK)],
+                      p_send.at[h, i], p_recv.at[h, i], after)
+
+    def partial_stats(h, i):
+        return remote(sn.at[h, i], sp.at[h, i], s_send.at[h, i], s_recv.at[h, i], after)
 
     def table_forward():
         return remote(table.at[pl.ds(ROW, ROW)], table.at[pl.ds(0, ROW)], idf_send, idf_recv, after)
@@ -143,7 +146,7 @@
         when(has_next, lambda: forward(t, h).start())
 
     def pass_back(h):
-        await_bytes(qb.at[h, pl.ds(0, BACKED)], q_recv.at[0, h])
+        await_bytes(qb.at[h], q_recv.at[h])
         when(has_prev, lambda: backward(h).start())
 
     for copy in id_copies:
@@ -182,28 +185,30 @@
         return jnp.dot(weights, values, preferred_element_type=jnp.float32)
 
     def block(i):
-        return pl.ds(pl.multiple_of(i * BLK, BLK), BLK)
-
-    def loop(body):
+        return pl.ds(i * BLK if isinstance(i, int) else pl.multiple_of(i * BLK, BLK), BLK)
+
+    def loop(count, body):
         def step(i, carry):
             body(i)
             return carry
 
-        lax.fori_loop(0, BACK, step, 0)
-
-    near = pl.ds(SPAN, BACKED)
-    front = pl.ds(BACKED, SPAN)
+        lax.fori_loop(0, count, step, 0)
+
+    def window(i):
+        return pl.ds(i * BLK if isinstance(i, int) else pl.multiple_of(i * BLK, BLK), WINDOW)
+
+    def front(h, i):
+        return pl.ds(BACK[h] * BLK, (ROW + 1 + i - BACK[h]) * BLK)
 
     def partial(h):
-        def body(i):
-            highest, total, weights = weigh(qn[h, block(i)], kv[0, h, near], bias_n[i])
-            on[h, block(i)] = blend(weights, kv[1, h, near]).astype(jnp.bfloat16)
+        for i in range(BACK[h]):
+            rows = pl.ds(SPAN + i * BLK, (BACK[h] - i) * BLK)
+            highest, total, weights = weigh(qn[h, block(i)], kv[0, h, rows], bias_n[i, :, 0:rows.size])
+            on[h, block(i)] = blend(weights, kv[1, h, rows]).astype(jnp.bfloat16)
             lane = lax.broadcasted_iota(jnp.int32, (BLK, HD), 1)
             sn[h, i] = jnp.transpose(jnp.where(lane == 0, highest, total))[0:8]
-
-        loop(body)
-        partial_out(h).start()
-        partial_stats(h).start()
+            partial_out(h, i).start()
+            partial_stats(h, i).start()
 
     def give_back(h, i):
         columns = pl.ds(pl.multiple_of(HD * (HEADS * me + h), HD), HD)
@@ -219,19 +224,19 @@
                 pltpu.make_async_copy(rows, o_ref.at[:, columns], o_recv.at[h]).start()
 
     def weigh_first(h):
-        def body(i):
-            tops[i], totals[i], weights_a[i] = weigh(qb[h, block(i)], kv[0, h, front], bias_a[i])
-
-        loop(body)
+        for i in range(BACK[h]):
+            rows = front(h, i)
+            tops[i], totals[i], weights_a[i, :, 0:rows.size] = weigh(
+                qb[h, block(i)], kv[0, h, rows], bias[i, :, (BACK[h] - i) * BLK:])
 
     def blend_first(h):
-        def body(i):
-            outs[i] = blend(weights_a[i], kv[1, h, front])
-
-        loop(body)
+        for i in range(BACK[h]):
+            rows = front(h, i)
+            outs[i] = blend(weights_a[i, :, 0:rows.size], kv[1, h, rows])
 
     def merge(h):
-        def body(i):
+        for i in range(BACK[h]):
+            when(has_prev, lambda: partial_out(h, i).wait_recv(), lambda: partial_stats(h, i).wait_recv())
             stats = jnp.transpose(sp[h, i])
             highest, other = tops[i], stats[:, 0:1]
             top = jnp.maximum(highest, other)
@@ -241,22 +246,24 @@
             ob[h, block(i)] = (out / total).astype(jnp.bfloat16)
             give_back(h, i)
 
-        loop(body)
-
     def weigh_last(h):
+        for i in range(BACK[h], ROW):
+            _, totals[i], weights_b[i - BACK[h]] = weigh(qb[h, block(i)], kv[0, h, window(i)], bias[i])
+
+    def blend_last(h):
+        for i in range(BACK[h], ROW):
+            out = blend(weights_b[i - BACK[h]], kv[1, h, window(i)])
+            ob[h, block(i)] = (out / totals[i]).astype(jnp.bfloat16)
+            give_back(h, i)
+
+    def attend(h):
         def body(i):
-            _, totals[BACK + i], weights_b[i] = weigh(
-                qb[h, block(BACK + i)], kv[0, h, pl.ds(pl.multiple_of((BACK + i) * BLK, BLK), WINDOW)], bias_b[i])
-
-        loop(body)
-
-    def blend_last(h):
-        def body(i):
-            out = blend(weights_b[i], kv[1, h, pl.ds(pl.multiple_of((BACK + i) * BLK, BLK), WINDOW)])
-            ob[h, block(BACK + i)] = (out / totals[BACK + i]).astype(jnp.bfloat16)
-            give_back(h, BACK + i)
-
-        loop(body)
+            _, total, weights = weigh(qb[h, block(i)], kv[0, h, window(i)], bias[i])
+            out = blend(weights, kv[1, h, window(i)])
+            ob[h, block(i)] = (out / total).astype(jnp.bfloat16)
+            give_back(h, i)
+
+        loop(ROW, body)
 
     def await_keys(h):
         when(has_prev, lambda: forward(0, h).wait_recv())
@@ -264,11 +271,8 @@
     def await_values(h):
         when(has_prev, lambda: forward(1, h).wait_recv())
 
-    def await_last(h):
-        await_bytes(qb.at[h, pl.ds(BACKED, SPAN - BACKED)], q_recv.at[1, h])
-
-    def await_partial(h):
-        when(has_prev, lambda: partial_out(h).wait_recv(), lambda: partial_stats(h).wait_recv())
+    def await_queries(h):
+        await_bytes(qb.at[h], q_recv.at[h])
 
     def next_part(h):
         @pl.when(has_next)
@@ -276,56 +280,43 @@
             backward(h).wait_recv()
             partial(h)
 
-    pass_back(0)
     pass_on(0, 0)
-    when(has_next, lambda: table_backward().wait_recv())
+    when(has_prev, lambda: table_forward().wait_recv())
+    for i in range(ROW):
+        terms(bias, i, ROW + i, range(i, ROW + i + 1))
 
     @pl.when(has_next)
     def _():
-        for i in range(BACK):
-            terms(bias_n, i, 2 * ROW + i, range(ROW, ROW + BACK))
+        table_backward().wait_recv()
+        for i in range(MOST):
+            terms(bias_n, i, 2 * ROW + i, range(ROW + i, ROW + MOST))
 
     pass_on(1, 0)
-    next_part(0)
     pass_back(1)
-    when(has_prev, lambda: table_forward().wait_recv())
-    for i in range(BACK):
-        terms(bias_a, i, ROW + i, range(BACK, BACK + ROW))
     pass_on(0, 1)
-    await_keys(0)
-    weigh_first(0)
-    await_values(0)
-    blend_first(0)
     pass_on(1, 1)
     next_part(1)
     pass_back(2)
-    await_partial(0)
-    merge(0)
-    for i in range(BACK):
-        terms(bias_b, i, ROW + BACK + i, range(BACK + i, BACK + i + WIN + 1))
     pass_on(0, 2)
     await_keys(1)
+    weigh_last(1)
     weigh_first(1)
+    await_values(1)
+    blend_last(1)
+    blend_first(1)
+    merge(1)
     pass_on(1, 2)
     next_part(2)
-    await_values(1)
-    blend_first(1)
-    await_last(0)
-    weigh_last(0)
-    blend_last(0)
-    await_partial(1)
-    merge(1)
-    await_last(1)
-    weigh_last(1)
-    blend_last(1)
     await_keys(2)
+    weigh_last(2)
     weigh_first(2)
-    await_last(2)
-    weigh_last(2)
+    await_queries(0)
+    await_keys(0)
+    await_values(0)
+    attend(0)
     await_values(2)
+    blend_last(2)
     blend_first(2)
-    blend_last(2)
-    await_partial(2)
     merge(2)
 
     sent = (TEAM - 1) * SHARE
@@ -340,13 +331,15 @@
         for h in range(HEADS):
             forward(0, h).wait_send()
             forward(1, h).wait_send()
-            partial_out(h).wait_send()
-            partial_stats(h).wait_send()
+        for h in SPLIT:
+            for i in range(BACK[h]):
+                partial_out(h, i).wait_send()
+                partial_stats(h, i).wait_send()
 
     @pl.when(has_prev)
     def _():
         table_backward().wait_send()
-        for h in range(HEADS):
+        for h in SPLIT:
             backward(h).wait_send()
 
     for h in range(HEADS):
@@ -370,26 +363,25 @@
             pltpu.VMEM((2, HEADS, 2 * SPAN, HD), bf16),
             pltpu.VMEM((HEADS, SPAN, HD), bf16),
             pltpu.VMEM((HEADS, SPAN, HD), bf16),
-            pltpu.VMEM((HEADS, BACKED, HD), bf16),
-            pltpu.VMEM((HEADS, BACKED, HD), bf16),
-            pltpu.VMEM((HEADS, BACK, 8, BLK), jnp.float32),
-            pltpu.VMEM((HEADS, BACKED, HD), bf16),
-            pltpu.VMEM((HEADS, BACK, 8, BLK), jnp.float32),
-            pltpu.VMEM((BACK, BLK, SPAN), jnp.float32),
-            pltpu.VMEM((BACK, BLK, WINDOW), jnp.float32),
-            pltpu.VMEM((BACK, BLK, BACKED), jnp.float32),
-            pltpu.VMEM((BACK, BLK, 1), jnp.float32),
+            pltpu.VMEM((HEADS, MOST * BLK, HD), bf16),
+            pltpu.VMEM((HEADS, MOST * BLK, HD), bf16),
+            pltpu.VMEM((HEADS, MOST, 8, BLK), jnp.float32),
+            pltpu.VMEM((HEADS, MOST * BLK, HD), bf16),
+            pltpu.VMEM((HEADS, MOST, 8, BLK), jnp.float32),
+            pltpu.VMEM((ROW, BLK, WINDOW), jnp.float32),
+            pltpu.VMEM((MOST, BLK, MOST * BLK), jnp.float32),
+            pltpu.VMEM((MOST, BLK, 1), jnp.float32),
             pltpu.VMEM((ROW, BLK, 1), jnp.float32),
-            pltpu.VMEM((BACK, BLK, HD), jnp.float32),
-            pltpu.VMEM((BACK, BLK, SPAN), bf16),
-            pltpu.VMEM((BACK, BLK, WINDOW), bf16),
+            pltpu.VMEM((MOST, BLK, HD), jnp.float32),
+            pltpu.VMEM((MOST, BLK, SPAN), bf16),
+            pltpu.VMEM((ROW - min(BACK[h] for h in SPLIT), BLK, WINDOW), bf16),
             dma((3,)), dma((4,)), dma, dma, dma, dma,
-            dma((2, HEADS)), dma((2, HEADS)), dma((HEADS,)), dma((2, HEADS)),
             dma((2, HEADS)), dma((2, HEADS)), dma((HEADS,)), dma((HEADS,)),
-            dma((HEADS,)), dma((HEADS,)), dma((HEADS,)), dma((HEADS,)), dma((HEADS,)), dma((HEADS,)),
+            dma((2, HEADS)), dma((2, HEADS)), dma((HEADS,)), dma((HEADS,)),
+            dma((HEADS, MOST)), dma((HEADS, MOST)), dma((HEADS, MOST)), dma((HEADS, MOST)), dma((HEADS,)), dma((HEADS,)),
         ],
         compiler_params=pltpu.CompilerParams(
-            collective_id=0, has_side_effects=True, vmem_limit_bytes=60 * 1024 * 1024),
+            collective_id=0, has_side_effects=True, vmem_limit_bytes=53 * 1024 * 1024),
     )(queries, keys, values, clip_ids.reshape(1, BLK), group_ids.reshape(1, BLK), pair_kinds)
 
 

time: 52.3 us -> 48.7 us (0.931)
  Pallas kernels: 50.1 us -> 47 us
    pallas_call x1, Pallas kernels: 50.1 us -> 47 us  [shards(): pl.pallas_call(kernel, out_shape=jax.ShapeDtypeStruct(queries.shape, bf16...]
    unnamed x1 -> x7, local copies, waits for them, and re-layouts: 2.06 us -> 1.57 us
where the time goes in v3:
time: 48.7 us; the launch traced here: 48.6 us
  Pallas kernels  47 us (97%)
  local copies, waits for them, and re-layouts  1.57 us (3%)
    pallas_call x1, Pallas kernels, shards(): pl.pallas_call(kernel, out_shape=jax.ShapeDtypeStruct(queries.shape, bf16...  47 us
    unnamed x7, local copies, waits for them, and re-layouts  1.57 us

profile of v3, /device:TPU:161, one launch (start us, length us, event | category | flops | bytes accessed | tf_op | source)
XLA Modules:
  0.0 48.6 jit_solution(17597826728504534806)
XLA Ops:
  0.0 0.0 copy-start.1
  0.0 0.0 copy-start
  0.0 0.0 copy-start.2
  0.0 0.7 %copy-done.1 = s32[256]{0:T(256)S(1)} copy-done((s32[256]{0:T(256)S(1)}, s32[256]{0:T(256)}, u32[]{:S(2)}) %copy-start.1) | copy-done | bytes 1048
  0.7 0.0 copy-done
  0.7 0.0 copy-done.2
  0.7 47.0 %shard_map.64 = bf16[128,3072]{1,0:T(8,128)(2,1)S(1)} custom-call(bf16[128,3072]{1,0:T(8,128)(2,1)} %q_ref.1, bf16[128,3072]{1,0:T(8,128)(2,1)} %k_ref.1, bf16[128,3072]{1,0:T(8,128)(2,1)} %v_ref.1, s32[1,256]{1,0:T(1,128)S(1)} %bitcast.2, s32[1,256]{1,0:T(1,128)S(1)} %bitcast.3, s32[1,4]{1,0:T(1,128)S(1)} %copy-done.2), custom_call_target="tpu_custom_call" | custom-call | tf_op jit(solution)/shard_map/pallas_call | solution.py:355
  47.7 0.9 %copy.8 = bf16[128,3072]{1,0:T(8,128)(2,1)} copy(bf16[128,3072]{1,0:T(8,128)(2,1)S(1)} %shard_map.64) | data formatting | bytes 1572864
Async XLA Ops:
  0.0 0.7 %copy-start.1 = (s32[256]{0:T(256)S(1)}, s32[256]{0:T(256)}, u32[]{:S(2)}) copy-start(s32[256]{0:T(256)} %param.10) | copy-start | bytes 3076
  0.0 0.7 %copy-start = (s32[256]{0:T(256)S(1)}, s32[256]{0:T(256)}, u32[]{:S(2)}) copy-start(s32[256]{0:T(256)} %param.9) | copy-start | bytes 3076
  0.0 0.7 %copy-start.2 = (s32[1,4]{1,0:T(1,128)S(1)}, s32[1,4]{1,0:T(1,128)}, u32[]{:S(2)}) copy-start(s32[1,4]{1,0:T(1,128)} %kinds_ref.1) | copy-start | bytes 52

commit v4 on v3

--- a/solution.py
+++ b/solution.py
@@ -14,9 +14,10 @@
 HEADS = 3
 SPAN = ROW * BLK
 WINDOW = (WIN + 1) * BLK
-BACK = (0, 3, 3)
+BACK = (0, 3, 2)
 MOST = max(BACK)
 SPLIT = tuple(h for h in range(HEADS) if BACK[h])
+FIRST = (1, 0)
 MESH = pl.DeviceIdType.MESH
 FACTOR = 1.4426950408889634 * HD ** -0.5
 MASKED = -1e30
@@ -24,9 +25,9 @@
 
 def kernel(q_ref, k_ref, v_ref, clip_ref, group_ref, kinds_ref, o_ref,
            mine, table, kv, qb, ob, qn, on, sn, op, sp, bias, bias_n,
-           tops, totals, outs, weights_a, weights_b,
+           tops, totals, outs, weights_of,
            id_send, id_recv, idf_send, idf_recv, idb_send, idb_recv, x_send, x_recv, q_send, q_recv, y_send, y_recv,
-           qb_send, qb_recv, p_send, p_recv, s_send, s_recv, o_send, o_recv):
+           chip_recv, qb_send, qb_recv, p_send, p_recv, s_send, s_recv, o_send, o_recv):
     ctx = lax.axis_index("ctx")
     core = lax.axis_index("head")
     x = ctx % ROW
@@ -39,7 +40,12 @@
         return (base + place // 2, place % 2)
 
     after, before = (ctx + ROW, core), (ctx - ROW, core)
-    partners = [(me + step) % TEAM for step in (2, 6, 4, 3, 7, 5, 1)]
+
+    def place_on(chips, c):
+        return 2 * ((x + chips) % ROW) + c
+
+    sibling = 2 * x + 1 - core
+    partners = [place_on(chips, c) for c in (0, 1) for chips in (1, 2, 3)] + [sibling]
 
     barrier = pltpu.get_barrier_semaphore()
     for place in partners:
@@ -59,12 +65,17 @@
         mine[2 + d:3 + d] = jnp.full((1, BLK), kinds_ref[0, d], jnp.int32)
     mine[6:8] = jnp.zeros((2, BLK), jnp.int32)
 
+    for h in SPLIT:
+        op[h, BACK[h] * BLK:] = jnp.zeros((SPAN - BACK[h] * BLK, HD), jnp.bfloat16)
+        sp[h, BACK[h]:] = jnp.full((ROW - BACK[h], 8, BLK), MASKED, jnp.float32)
+
     @pl.when(jnp.logical_not(has_prev))
     def _():
         kv[:, :, 0:SPAN, :] = jnp.zeros((2, HEADS, SPAN, HD), jnp.bfloat16)
         table[0:ROW] = jnp.zeros((ROW, 8, BLK), jnp.int32)
-        op[...] = jnp.zeros((HEADS, MOST * BLK, HD), jnp.bfloat16)
-        sp[...] = jnp.full((HEADS, MOST, 8, BLK), MASKED, jnp.float32)
+        for h in SPLIT:
+            op[h, 0:BACK[h] * BLK] = jnp.zeros((BACK[h] * BLK, HD), jnp.bfloat16)
+            sp[h, 0:BACK[h]] = jnp.full((BACK[h], 8, BLK), MASKED, jnp.float32)
 
     pl.semaphore_wait(barrier, TEAM - 1 + jnp.where(has_next, 1, 0) + jnp.where(has_prev, 1, 0))
 
@@ -77,46 +88,64 @@
     own_ids = pltpu.make_async_copy(mine, table.at[ROW + x], id_recv.at[3])
     own_ids.start()
 
-    def share(ref, h, landing, send, recv):
-        def columns(place):
-            return pl.ds(pl.multiple_of(HD * (HEADS * place + h), HD), HD)
-
+    def remote(src, dst, send, recv, to):
+        return pltpu.make_async_remote_copy(src, dst, send, recv, device_id=to, device_id_type=MESH)
+
+    def share(ref, h, landing, send, recv, places):
         rows = pl.ds(pl.multiple_of(SHARE * me, SHARE), SHARE)
-        for place in partners:
-            pltpu.make_async_remote_copy(
-                ref.at[:, columns(place)], landing.at[rows], send, recv,
-                device_id=device(place), device_id_type=MESH).start()
-        pltpu.make_async_copy(ref.at[:, columns(me)], landing.at[rows], recv).start()
+        for place in places:
+            source = ref.at[:, pl.ds(pl.multiple_of(HD * (HEADS * place + h), HD), HD)]
+            if place is me:
+                pltpu.make_async_copy(source, landing.at[rows], recv).start()
+            else:
+                remote(source, landing.at[rows], send, recv, device(place)).start()
 
     own = pl.ds(SPAN, SPAN)
-
-    def share_key(h):
-        share(k_ref, h, kv.at[0, h, own], x_send.at[0, h], x_recv.at[0, h])
-
-    def share_value(h):
-        share(v_ref, h, kv.at[1, h, own], x_send.at[1, h], x_recv.at[1, h])
-
-    def share_query(h):
-        share(q_ref, h, qb.at[h], q_send.at[h], q_recv.at[h])
-
-    share_key(0)
-    share_value(0)
+    here = (sibling, me)
+    away = [place_on(chips, c) for c in FIRST for chips in (1, 3, 2)]
+    everywhere = [*away, *here]
+
+    def share_key(h, part, steps=everywhere):
+        share(k_ref, h, kv.at[0, h, own], x_send.at[0, h], x_recv.at[0, h, part], steps)
+
+    def share_value(h, part, steps=everywhere):
+        share(v_ref, h, kv.at[1, h, own], x_send.at[1, h], x_recv.at[1, h, part], steps)
+
+    def share_query(h, part):
+        share(q_ref, h, qb.at[h], q_send.at[h], q_recv.at[h, part], everywhere)
+
+    share_key(0, 0, here)
+    share_value(0, 0, here)
+    share_key(0, 1, away)
+    share_value(0, 1, away)
+    share(q_ref, 0, qb.at[0], q_send.at[0], chip_recv.at[0], here)
     for h in SPLIT:
-        share_query(h)
-        share_key(h)
-        share_value(h)
-    share_query(0)
+        @pl.when(x < BACK[h])
+        def _():
+            share_query(h, 0)
+            share_key(h, 0)
+            share_value(h, 0)
+
+        @pl.when(x >= BACK[h])
+        def _():
+            share_key(h, 1)
+            share_value(h, 1)
+            share_query(h, 1)
+
+    for chips in (1, 3, 2):
+        share(q_ref, 0, qb.at[0], q_send.at[0], chip_recv.at[chips], [place_on(chips, c) for c in FIRST])
 
     def await_bytes(ref, sem):
         pltpu.make_async_copy(ref, ref, sem).wait()
-
-    def remote(src, dst, send, recv, to):
-        return pltpu.make_async_remote_copy(src, dst, send, recv, device_id=to, device_id_type=MESH)
 
     def forward(t, h):
         first = BACK[h] * BLK
         return remote(kv.at[t, h, pl.ds(SPAN + first, SPAN - first)], kv.at[t, h, pl.ds(first, SPAN - first)],
                       y_send.at[t, h], y_recv.at[t, h], after)
+
+    def forward_block(t, i):
+        rows = pl.ds(pl.multiple_of(i * BLK, BLK), BLK)
+        return remote(kv.at[t, 0, own].at[rows], kv.at[t, 0, rows], y_send.at[t, 0], y_recv.at[t, 0], after)
 
     def backward(h):
         first = pl.ds(0, BACK[h] * BLK)
@@ -141,13 +170,34 @@
             for action in actions:
                 action()
 
+    def first_rows(h):
+        return pl.ds(0, BACK[h] * BLK)
+
+    def last_rows(h):
+        return pl.ds(BACK[h] * BLK, SPAN - BACK[h] * BLK)
+
     def pass_on(t, h):
-        await_bytes(kv.at[t, h, own], x_recv.at[t, h])
+        await_bytes(kv.at[t, h, last_rows(h)], x_recv.at[t, h, 1])
         when(has_next, lambda: forward(t, h).start())
 
+    def pass_own(t):
+        await_bytes(kv.at[t, 0, pl.ds(0, BLK)], x_recv.at[t, 0, 0])
+        when(has_next, lambda: forward_block(t, x).start())
+
+    def pass_rest(t):
+        await_bytes(kv.at[t, 0, pl.ds(0, SPAN - BLK)], x_recv.at[t, 0, 1])
+        when(has_next, *[lambda n=n: forward_block(t, (x + n) % ROW).start() for n in (1, 3, 2)])
+
     def pass_back(h):
-        await_bytes(qb.at[h], q_recv.at[h])
+        await_bytes(qb.at[h, first_rows(h)], q_recv.at[h, 0])
         when(has_prev, lambda: backward(h).start())
+
+    def await_first(h):
+        for t in range(2):
+            await_bytes(kv.at[t, h, first_rows(h)], x_recv.at[t, h, 0])
+
+    def await_last(h):
+        await_bytes(qb.at[h, last_rows(h)], q_recv.at[h, 1])
 
     for copy in id_copies:
         copy.wait()
@@ -174,9 +224,11 @@
         for n, slot in enumerate(slots):
             ref[i, :, n * BLK:(n + 1) * BLK] = pair(query_slot, slot)
 
-    def weigh(queries, keys, term):
-        scores = lax.dot_general(queries, keys, (((1,), (1,)), ((), ())), preferred_element_type=jnp.float32)
-        scores = scores + term
+    def score(queries, keys, term):
+        return lax.dot_general(
+            queries, keys, (((1,), (1,)), ((), ())), preferred_element_type=jnp.float32) + term
+
+    def weigh(scores):
         highest = jnp.max(scores, axis=1, keepdims=True)
         weights = jnp.exp2((scores - highest) * FACTOR)
         return highest, jnp.sum(weights, axis=1, keepdims=True), weights.astype(jnp.bfloat16)
@@ -187,24 +239,25 @@
     def block(i):
         return pl.ds(i * BLK if isinstance(i, int) else pl.multiple_of(i * BLK, BLK), BLK)
 
-    def loop(count, body):
-        def step(i, carry):
-            body(i)
-            return carry
-
-        lax.fori_loop(0, count, step, 0)
-
-    def window(i):
-        return pl.ds(i * BLK if isinstance(i, int) else pl.multiple_of(i * BLK, BLK), WINDOW)
-
-    def front(h, i):
-        return pl.ds(BACK[h] * BLK, (ROW + 1 + i - BACK[h]) * BLK)
+    def window(h, i):
+        if isinstance(i, int) and i < BACK[h]:
+            return pl.ds(BACK[h] * BLK, (ROW + 1 + i - BACK[h]) * BLK)
+        return pl.ds(block(i).start, WINDOW)
 
     def partial(h):
-        for i in range(BACK[h]):
-            rows = pl.ds(SPAN + i * BLK, (BACK[h] - i) * BLK)
-            highest, total, weights = weigh(qn[h, block(i)], kv[0, h, rows], bias_n[i, :, 0:rows.size])
-            on[h, block(i)] = blend(weights, kv[1, h, rows]).astype(jnp.bfloat16)
+        def rows(i):
+            return pl.ds(SPAN + i * BLK, (BACK[h] - i) * BLK)
+
+        def scores(i):
+            return score(qn[h, block(i)], kv[0, h, rows(i)], bias_n[i, :, i * BLK:BACK[h] * BLK])
+
+        following = scores(BACK[h] - 1)
+        for i in reversed(range(BACK[h])):
+            current = following
+            if i:
+                following = scores(i - 1)
+            highest, total, weights = weigh(current)
+            on[h, block(i)] = blend(weights, kv[1, h, rows(i)]).astype(jnp.bfloat16)
             lane = lax.broadcasted_iota(jnp.int32, (BLK, HD), 1)
             sn[h, i] = jnp.transpose(jnp.where(lane == 0, highest, total))[0:8]
             partial_out(h, i).start()
@@ -223,20 +276,32 @@
             def _():
                 pltpu.make_async_copy(rows, o_ref.at[:, columns], o_recv.at[h]).start()
 
-    def weigh_first(h):
-        for i in range(BACK[h]):
-            rows = front(h, i)
-            tops[i], totals[i], weights_a[i, :, 0:rows.size] = weigh(
-                qb[h, block(i)], kv[0, h, rows], bias[i, :, (BACK[h] - i) * BLK:])
-
-    def blend_first(h):
-        for i in range(BACK[h]):
-            rows = front(h, i)
-            outs[i] = blend(weights_a[i, :, 0:rows.size], kv[1, h, rows])
+    def weigh_all(h):
+        def scores(i):
+            first = (BACK[h] - i) * BLK if i < BACK[h] else 0
+            return score(qb[h, block(i)], kv[0, h, window(h, i)], bias[i, :, first:])
+
+        following = scores(0)
+        for i in range(ROW):
+            current = following
+            if i + 1 < ROW:
+                following = scores(i + 1)
+            tops[i], totals[i], weights_of[i, :, 0:window(h, i).size] = weigh(current)
+
+    def blend_all(h):
+        for i in range(ROW):
+            rows = window(h, i)
+            outs[i] = blend(weights_of[i, :, 0:rows.size], kv[1, h, rows])
 
     def merge(h):
-        for i in range(BACK[h]):
-            when(has_prev, lambda: partial_out(h, i).wait_recv(), lambda: partial_stats(h, i).wait_recv())
+        def body(n, carry):
+            i = (x + 1 + n) % ROW
+
+            @pl.when(has_prev & (i < BACK[h]))
+            def _():
+                partial_out(h, i).wait_recv()
+                partial_stats(h, i).wait_recv()
+
             stats = jnp.transpose(sp[h, i])
             highest, other = tops[i], stats[:, 0:1]
             top = jnp.maximum(highest, other)
@@ -245,34 +310,31 @@
             out = outs[i] * here + op[h, block(i)].astype(jnp.float32) * there
             ob[h, block(i)] = (out / total).astype(jnp.bfloat16)
             give_back(h, i)
-
-    def weigh_last(h):
-        for i in range(BACK[h], ROW):
-            _, totals[i], weights_b[i - BACK[h]] = weigh(qb[h, block(i)], kv[0, h, window(i)], bias[i])
-
-    def blend_last(h):
-        for i in range(BACK[h], ROW):
-            out = blend(weights_b[i - BACK[h]], kv[1, h, window(i)])
-            ob[h, block(i)] = (out / totals[i]).astype(jnp.bfloat16)
-            give_back(h, i)
-
-    def attend(h):
-        def body(i):
-            _, total, weights = weigh(qb[h, block(i)], kv[0, h, window(i)], bias[i])
-            out = blend(weights, kv[1, h, window(i)])
-            ob[h, block(i)] = (out / total).astype(jnp.bfloat16)
-            give_back(h, i)
-
-        loop(ROW, body)
+            return carry
+
+        lax.fori_loop(0, ROW, body, 0)
+
+    def attend(*distances):
+        def scores(chips):
+            i = (x + ROW - chips) % ROW
+            await_bytes(qb.at[0, block(i)], chip_recv.at[chips])
+            return i, score(qb[0, block(i)], kv[0, 0, window(0, i)], bias[i])
+
+        following = scores(distances[0])
+        for n in range(len(distances)):
+            i, current = following
+            if n + 1 < len(distances):
+                following = scores(distances[n + 1])
+            _, total, weights = weigh(current)
+            out = blend(weights, kv[1, 0, window(0, i)])
+            ob[0, block(i)] = (out / total).astype(jnp.bfloat16)
+            give_back(0, i)
 
     def await_keys(h):
         when(has_prev, lambda: forward(0, h).wait_recv())
 
     def await_values(h):
         when(has_prev, lambda: forward(1, h).wait_recv())
-
-    def await_queries(h):
-        await_bytes(qb.at[h], q_recv.at[h])
 
     def next_part(h):
         @pl.when(has_next)
@@ -280,7 +342,9 @@
             backward(h).wait_recv()
             partial(h)
 
-    pass_on(0, 0)
+    pass_own(0)
+    pass_own(1)
+    pass_rest(0)
     when(has_prev, lambda: table_forward().wait_recv())
     for i in range(ROW):
         terms(bias, i, ROW + i, range(i, ROW + i + 1))
@@ -289,34 +353,34 @@
     def _():
         table_backward().wait_recv()
         for i in range(MOST):
-            terms(bias_n, i, 2 * ROW + i, range(ROW + i, ROW + MOST))
-
-    pass_on(1, 0)
+            terms(bias_n, i, 2 * ROW + i, range(ROW, ROW + MOST))
+
+    pass_rest(1)
     pass_back(1)
     pass_on(0, 1)
     pass_on(1, 1)
+    await_first(1)
     next_part(1)
     pass_back(2)
     pass_on(0, 2)
+    await_last(1)
     await_keys(1)
-    weigh_last(1)
-    weigh_first(1)
+    weigh_all(1)
+    pass_on(1, 2)
     await_values(1)
-    blend_last(1)
-    blend_first(1)
-    merge(1)
-    pass_on(1, 2)
-    next_part(2)
-    await_keys(2)
-    weigh_last(2)
-    weigh_first(2)
-    await_queries(0)
+    blend_all(1)
     await_keys(0)
     await_values(0)
     attend(0)
+    await_first(2)
+    next_part(2)
+    merge(1)
+    await_last(2)
+    await_keys(2)
+    weigh_all(2)
+    attend(1, 3, 2)
     await_values(2)
-    blend_last(2)
-    blend_first(2)
+    blend_all(2)
     merge(2)
 
     sent = (TEAM - 1) * SHARE
@@ -366,18 +430,17 @@
             pltpu.VMEM((HEADS, MOST * BLK, HD), bf16),
             pltpu.VMEM((HEADS, MOST * BLK, HD), bf16),
             pltpu.VMEM((HEADS, MOST, 8, BLK), jnp.float32),
-            pltpu.VMEM((HEADS, MOST * BLK, HD), bf16),
-            pltpu.VMEM((HEADS, MOST, 8, BLK), jnp.float32),
+            pltpu.VMEM((HEADS, SPAN, HD), bf16),
+            pltpu.VMEM((HEADS, ROW, 8, BLK), jnp.float32),
             pltpu.VMEM((ROW, BLK, WINDOW), jnp.float32),
             pltpu.VMEM((MOST, BLK, MOST * BLK), jnp.float32),
-            pltpu.VMEM((MOST, BLK, 1), jnp.float32),
             pltpu.VMEM((ROW, BLK, 1), jnp.float32),
-            pltpu.VMEM((MOST, BLK, HD), jnp.float32),
-            pltpu.VMEM((MOST, BLK, SPAN), bf16),
-            pltpu.VMEM((ROW - min(BACK[h] for h in SPLIT), BLK, WINDOW), bf16),
+            pltpu.VMEM((ROW, BLK, 1), jnp.float32),
+            pltpu.VMEM((ROW, BLK, HD), jnp.float32),
+            pltpu.VMEM((ROW, BLK, WINDOW), bf16),
             dma((3,)), dma((4,)), dma, dma, dma, dma,
-            dma((2, HEADS)), dma((2, HEADS)), dma((HEADS,)), dma((HEADS,)),
-            dma((2, HEADS)), dma((2, HEADS)), dma((HEADS,)), dma((HEADS,)),
+            dma((2, HEADS)), dma((2, HEADS, 2)), dma((HEADS,)), dma((HEADS, 2)),
+            dma((2, HEADS)), dma((2, HEADS)), dma((ROW,)), dma((HEADS,)), dma((HEADS,)),
             dma((HEADS, MOST)), dma((HEADS, MOST)), dma((HEADS, MOST)), dma((HEADS, MOST)), dma((HEADS,)), dma((HEADS,)),
         ],
         compiler_params=pltpu.CompilerParams(

time: 48.7 us -> 47 us (0.965)
  Pallas kernels: 47 us -> 45.4 us
    pallas_call x1, Pallas kernels: 47 us -> 45.4 us  [shards(): pl.pallas_call(kernel, out_shape=jax.ShapeDtypeStruct(queries.shape, bf16...]
where the time goes in v4:
time: 47 us
  Pallas kernels  45.4 us (97%)
  local copies, waits for them, and re-layouts  1.57 us (3%)
    pallas_call x1, Pallas kernels, shards(): pl.pallas_call(kernel, out_shape=jax.ShapeDtypeStruct(queries.shape, bf16...  45.4 us
    unnamed x7, local copies, waits for them, and re-layouts  1.57 us

profile of v4, /device:TPU:161, one launch (start us, length us, event | category | flops | bytes accessed | tf_op | source)
XLA Modules:
  0.0 47.0 jit_solution(11626417640137228270)
XLA Ops:
  0.0 0.0 copy-start.1
  0.0 0.0 copy-start
  0.0 0.0 copy-start.2
  0.0 0.7 %copy-done.1 = s32[256]{0:T(256)S(1)} copy-done((s32[256]{0:T(256)S(1)}, s32[256]{0:T(256)}, u32[]{:S(2)}) %copy-start.1) | copy-done | bytes 1048
  0.7 0.0 copy-done
  0.7 0.0 copy-done.2
  0.7 45.4 %shard_map.64 = bf16[128,3072]{1,0:T(8,128)(2,1)S(1)} custom-call(bf16[128,3072]{1,0:T(8,128)(2,1)} %q_ref.1, bf16[128,3072]{1,0:T(8,128)(2,1)} %k_ref.1, bf16[128,3072]{1,0:T(8,128)(2,1)} %v_ref.1, s32[1,256]{1,0:T(1,128)S(1)} %bitcast.2, s32[1,256]{1,0:T(1,128)S(1)} %bitcast.3, s32[1,4]{1,0:T(1,128)S(1)} %copy-done.2), custom_call_target="tpu_custom_call" | custom-call | tf_op jit(solution)/shard_map/pallas_call | solution.py:419
  46.1 0.9 %copy.8 = bf16[128,3072]{1,0:T(8,128)(2,1)} copy(bf16[128,3072]{1,0:T(8,128)(2,1)S(1)} %shard_map.64) | data formatting | bytes 1572864
Async XLA Ops:
  0.0 0.7 %copy-start.1 = (s32[256]{0:T(256)S(1)}, s32[256]{0:T(256)}, u32[]{:S(2)}) copy-start(s32[256]{0:T(256)} %param.10) | copy-start | bytes 3076
  0.0 0.7 %copy-start = (s32[256]{0:T(256)S(1)}, s32[256]{0:T(256)}, u32[]{:S(2)}) copy-start(s32[256]{0:T(256)} %param.9) | copy-start | bytes 3076
  0.0 0.7 %copy-start.2 = (s32[1,4]{1,0:T(1,128)S(1)}, s32[1,4]{1,0:T(1,128)}, u32[]{:S(2)}) copy-start(s32[1,4]{1,0:T(1,128)} %kinds_ref.1) | copy-start | bytes 52

commit v5 on v4

--- a/solution.py
+++ b/solution.py
@@ -14,7 +14,7 @@
 HEADS = 3
 SPAN = ROW * BLK
 WINDOW = (WIN + 1) * BLK
-BACK = (0, 3, 2)
+BACK = (0, 3, 3)
 MOST = max(BACK)
 SPLIT = tuple(h for h in range(HEADS) if BACK[h])
 FIRST = (1, 0)
@@ -265,7 +265,7 @@
 
     def give_back(h, i):
         columns = pl.ds(pl.multiple_of(HD * (HEADS * me + h), HD), HD)
-        for place in (2 * i, 2 * i + 1):
+        for place in (2 * i + 1, 2 * i):
             rows = ob.at[h, pl.ds(pl.multiple_of(SHARE * place, SHARE), SHARE)]
 
             @pl.when(me != place)
@@ -371,17 +371,17 @@
     blend_all(1)
     await_keys(0)
     await_values(0)
-    attend(0)
     await_first(2)
     next_part(2)
     merge(1)
+    attend(1, 3, 2)
     await_last(2)
     await_keys(2)
     weigh_all(2)
-    attend(1, 3, 2)
     await_values(2)
     blend_all(2)
     merge(2)
+    attend(0)
 
     sent = (TEAM - 1) * SHARE
     for h in range(HEADS):

time: 47 us -> 46 us (0.979)
  Pallas kernels: 45.4 us -> 44.1 us
    pallas_call x1, Pallas kernels: 45.4 us -> 44.1 us  [shards(): pl.pallas_call(kernel, out_shape=jax.ShapeDtypeStruct(queries.shape, bf16...]
where the time goes in v5:
time: 46 us; the launch traced here: 45.6 us
  Pallas kernels  44.1 us (96%)
  local copies, waits for them, and re-layouts  1.57 us (3%)
    pallas_call x1, Pallas kernels, shards(): pl.pallas_call(kernel, out_shape=jax.ShapeDtypeStruct(queries.shape, bf16...  44.1 us
    unnamed x7, local copies, waits for them, and re-layouts  1.57 us

profile of v5, /device:TPU:161, one launch (start us, length us, event | category | flops | bytes accessed | tf_op | source)
XLA Modules:
  0.0 45.6 jit_solution(9542918510767330727)
XLA Ops:
  0.0 0.0 copy-start.1
  0.0 0.0 copy-start
  0.0 0.0 copy-start.2
  0.0 0.7 %copy-done.1 = s32[256]{0:T(256)S(1)} copy-done((s32[256]{0:T(256)S(1)}, s32[256]{0:T(256)}, u32[]{:S(2)}) %copy-start.1) | copy-done | bytes 1048
  0.7 0.0 copy-done
  0.7 0.0 copy-done.2
  0.7 44.1 %shard_map.64 = bf16[128,3072]{1,0:T(8,128)(2,1)S(1)} custom-call(bf16[128,3072]{1,0:T(8,128)(2,1)} %q_ref.1, bf16[128,3072]{1,0:T(8,128)(2,1)} %k_ref.1, bf16[128,3072]{1,0:T(8,128)(2,1)} %v_ref.1, s32[1,256]{1,0:T(1,128)S(1)} %bitcast.2, s32[1,256]{1,0:T(1,128)S(1)} %bitcast.3, s32[1,4]{1,0:T(1,128)S(1)} %copy-done.2), custom_call_target="tpu_custom_call" | custom-call | tf_op jit(solution)/shard_map/pallas_call | solution.py:419
  44.8 0.9 %copy.8 = bf16[128,3072]{1,0:T(8,128)(2,1)} copy(bf16[128,3072]{1,0:T(8,128)(2,1)S(1)} %shard_map.64) | data formatting | bytes 1572864
Async XLA Ops:
  0.0 0.7 %copy-start.1 = (s32[256]{0:T(256)S(1)}, s32[256]{0:T(256)}, u32[]{:S(2)}) copy-start(s32[256]{0:T(256)} %param.10) | copy-start | bytes 3076
  0.0 0.7 %copy-start = (s32[256]{0:T(256)S(1)}, s32[256]{0:T(256)}, u32[]{:S(2)}) copy-start(s32[256]{0:T(256)} %param.9) | copy-start | bytes 3076
  0.0 0.7 %copy-start.2 = (s32[1,4]{1,0:T(1,128)S(1)}, s32[1,4]{1,0:T(1,128)}, u32[]{:S(2)}) copy-start(s32[1,4]{1,0:T(1,128)} %kinds_ref.1) | copy-start | bytes 52

commit v6 on v5

--- a/solution.py
+++ b/solution.py
@@ -102,7 +102,7 @@
 
     own = pl.ds(SPAN, SPAN)
     here = (sibling, me)
-    away = [place_on(chips, c) for c in FIRST for chips in (1, 3, 2)]
+    away = [place_on(chips, c) for c in FIRST for chips in (2, 1, 3)]
     everywhere = [*away, *here]
 
     def share_key(h, part, steps=everywhere):

time: 46 us -> 45.8 us (level); the launches traced: 45.6 us -> 44.8 us
  Pallas kernels: 44.1 us -> 43.2 us
    pallas_call x1, Pallas kernels: 44.1 us -> 43.2 us  [shards(): pl.pallas_call(kernel, out_shape=jax.ShapeDtypeStruct(queries.shape, bf16...]
where the time goes in v6:
time: 45.8 us; the launch traced here: 44.8 us
  Pallas kernels  43.2 us (94%)
  local copies, waits for them, and re-layouts  1.57 us (3%)
    pallas_call x1, Pallas kernels, shards(): pl.pallas_call(kernel, out_shape=jax.ShapeDtypeStruct(queries.shape, bf16...  43.2 us
    unnamed x7, local copies, waits for them, and re-layouts  1.57 us

profile of v6, /device:TPU:161, one launch (start us, length us, event | category | flops | bytes accessed | tf_op | source)
XLA Modules:
  0.0 44.8 jit_solution(3979745036091937776)
XLA Ops:
  0.0 0.0 copy-start.1
  0.0 0.0 copy-start
  0.0 0.0 copy-start.2
  0.0 0.7 %copy-done.1 = s32[256]{0:T(256)S(1)} copy-done((s32[256]{0:T(256)S(1)}, s32[256]{0:T(256)}, u32[]{:S(2)}) %copy-start.1) | copy-done | bytes 1048
  0.7 0.0 copy-done
  0.7 0.0 copy-done.2
  0.7 43.2 %shard_map.64 = bf16[128,3072]{1,0:T(8,128)(2,1)S(1)} custom-call(bf16[128,3072]{1,0:T(8,128)(2,1)} %q_ref.1, bf16[128,3072]{1,0:T(8,128)(2,1)} %k_ref.1, bf16[128,3072]{1,0:T(8,128)(2,1)} %v_ref.1, s32[1,256]{1,0:T(1,128)S(1)} %bitcast.2, s32[1,256]{1,0:T(1,128)S(1)} %bitcast.3, s32[1,4]{1,0:T(1,128)S(1)} %copy-done.2), custom_call_target="tpu_custom_call" | custom-call | tf_op jit(solution)/shard_map/pallas_call | solution.py:419
  44.0 0.9 %copy.8 = bf16[128,3072]{1,0:T(8,128)(2,1)} copy(bf16[128,3072]{1,0:T(8,128)(2,1)S(1)} %shard_map.64) | data formatting | bytes 1572864
Async XLA Ops:
  0.0 0.7 %copy-start.1 = (s32[256]{0:T(256)S(1)}, s32[256]{0:T(256)}, u32[]{:S(2)}) copy-start(s32[256]{0:T(256)} %param.10) | copy-start | bytes 3076
  0.0 0.7 %copy-start = (s32[256]{0:T(256)S(1)}, s32[256]{0:T(256)}, u32[]{:S(2)}) copy-start(s32[256]{0:T(256)} %param.9) | copy-start | bytes 3076
  0.0 0.7 %copy-start.2 = (s32[1,4]{1,0:T(1,128)S(1)}, s32[1,4]{1,0:T(1,128)}, u32[]{:S(2)}) copy-start(s32[1,4]{1,0:T(1,128)} %kinds_ref.1) | copy-start | bytes 52

commit v7 on v6

--- a/solution.py
+++ b/solution.py
@@ -295,7 +295,7 @@
 
     def merge(h):
         def body(n, carry):
-            i = (x + 1 + n) % ROW
+            i = (x + jnp.where(n < 2, 2 - n, (n + 1) % ROW)) % ROW
 
             @pl.when(has_prev & (i < BACK[h]))
             def _():

time: 45.8 us -> 45.7 us (level)
  no operation moved by 1% of the time
where the time goes in v7:
time: 45.7 us; the launch traced here: 45.2 us
  Pallas kernels  43.6 us (95%)
  local copies, waits for them, and re-layouts  1.57 us (3%)
    pallas_call x1, Pallas kernels, shards(): pl.pallas_call(kernel, out_shape=jax.ShapeDtypeStruct(queries.shape, bf16...  43.6 us
    unnamed x7, local copies, waits for them, and re-layouts  1.57 us

profile of v7, /device:TPU:161, one launch (start us, length us, event | category | flops | bytes accessed | tf_op | source)
XLA Modules:
  0.0 45.2 jit_solution(4904626252239267117)
XLA Ops:
  0.0 0.0 copy-start.1
  0.0 0.0 copy-start
  0.0 0.0 copy-start.2
  0.0 0.7 %copy-done.1 = s32[256]{0:T(256)S(1)} copy-done((s32[256]{0:T(256)S(1)}, s32[256]{0:T(256)}, u32[]{:S(2)}) %copy-start.1) | copy-done | bytes 1048
  0.7 0.0 copy-done
  0.7 0.0 copy-done.2
  0.7 43.6 %shard_map.64 = bf16[128,3072]{1,0:T(8,128)(2,1)S(1)} custom-call(bf16[128,3072]{1,0:T(8,128)(2,1)} %q_ref.1, bf16[128,3072]{1,0:T(8,128)(2,1)} %k_ref.1, bf16[128,3072]{1,0:T(8,128)(2,1)} %v_ref.1, s32[1,256]{1,0:T(1,128)S(1)} %bitcast.2, s32[1,256]{1,0:T(1,128)S(1)} %bitcast.3, s32[1,4]{1,0:T(1,128)S(1)} %copy-done.2), custom_call_target="tpu_custom_call" | custom-call | tf_op jit(solution)/shard_map/pallas_call | solution.py:419
  44.3 0.9 %copy.8 = bf16[128,3072]{1,0:T(8,128)(2,1)} copy(bf16[128,3072]{1,0:T(8,128)(2,1)S(1)} %shard_map.64) | data formatting | bytes 1572864
Async XLA Ops:
  0.0 0.7 %copy-start.1 = (s32[256]{0:T(256)S(1)}, s32[256]{0:T(256)}, u32[]{:S(2)}) copy-start(s32[256]{0:T(256)} %param.10) | copy-start | bytes 3076
  0.0 0.7 %copy-start = (s32[256]{0:T(256)S(1)}, s32[256]{0:T(256)}, u32[]{:S(2)}) copy-start(s32[256]{0:T(256)} %param.9) | copy-start | bytes 3076
  0.0 0.7 %copy-start.2 = (s32[1,4]{1,0:T(1,128)S(1)}, s32[1,4]{1,0:T(1,128)}, u32[]{:S(2)}) copy-start(s32[1,4]{1,0:T(1,128)} %kinds_ref.1) | copy-start | bytes 52
